TPU v7x, 256 devices: a whole 4x4x8 slice. The times are simulated.
256 devices in a mesh: ta: 4 (over y), xyz: 64 (over z, x, core).
Axes of the slice: x: 4, y: 4, z: 8, core: 2. Of those that a mesh axis runs over, the one named last changes fastest.
Arguments:
- vectors: bfloat16 [8, 3, 32768, 128], P('ta', None, 'xyz'), parts along dimension 0, may hold values from -6 to 6
- links: bfloat16 [12, 2, 3, 3, 32768], P('ta', None, None, None, 'xyz'), parts along dimension 0, may hold values from -2.5 to 2.5
- momenta: int32 [2, 3], replicated, may hold values from -2 to 2
- directions: int32 [3], replicated, may hold values from 0 to 2, each once
Outputs:
- elementals: float32 [8, 3, 2, 128, 128], P('ta', None, None, 'xyz'), parts along dimension 0
There are 4 independent parts, one for each index of `ta`. A program takes and returns all parts, laid end to end along the dimension named above; an argument that names none is the same for every part. Nothing has to cross between parts.
Inputs may be any that keep to these rules, and one draw needn't show every extreme that they name: `directions`: each lattice direction appears once.
All inputs are finite; a program needn't handle non-finite values.
Results may differ from a plain program's by a relative error of at most 0.0039.
Values may be sent and summed in bfloat16 or wider, within the bound.
No kernel may reach another device: no remote copies, remote signals or barrier semaphores. Data moves between devices by JAX's collectives and lax.ppermute only.
A program may use at most 64 MiB of HBM per device.

v0:
```python
import math

import jax
import jax.numpy as jnp
from jax import lax
from jax.sharding import PartitionSpec as P

SIDE = 8


def passed_along(value, axis, steps):
    count = lax.axis_size(axis)
    pairs = [(source, (source + steps) % count) for source in range(count)]
    return lax.ppermute(value, axis, pairs)


def neighbour_face(boundary, lattice_dim, stride, blocks, position, sense):
    if lattice_dim == 0:
        return passed_along(boundary, "xyz", -stride)
    forward = passed_along(boundary, "xyz", -sense * stride)
    beside_all = passed_along(boundary, "xyz", sense * (blocks - 1) * stride)
    return jnp.where(position == blocks - 1, beside_all, forward)


def make_terms(left_piece, combined):
    per_shift = [
        jnp.einsum(
            "rcsma,rcsob->aomb",
            left_piece,
            combined[:, :, :, :, shift_dim],
            preferred_element_type=jnp.float32,
        )
        for shift_dim in range(3)
    ]
    terms = jnp.stack(per_shift, axis=2)
    return terms


def per_device(vectors, links, momenta, directions):
    members = lax.axis_size("xyz")
    blocks = int(members ** (1.0 / 3.0) + 0.5)
    vec_count = vectors.shape[3]
    site_count = vectors.shape[2]
    my_index = lax.axis_index("xyz")
    positions = (
        my_index // (blocks * blocks),
        blocks - 1 - my_index // blocks % blocks,
        my_index % blocks,
    )
    strides = (blocks * blocks, blocks, 1)
    senses = (1, -1, 1)
    lattice_block = vectors.reshape(2, 3, SIDE, SIDE, SIDE, vec_count)
    displaced = []
    for lattice_dim in range(3):
        boundary = lax.slice_in_dim(lattice_block, 0, 1, axis=2 + lattice_dim)
        arrived = neighbour_face(
            boundary,
            lattice_dim,
            strides[lattice_dim],
            blocks,
            positions[lattice_dim],
            senses[lattice_dim],
        )
        inner_part = lax.slice_in_dim(lattice_block, 1, SIDE, axis=2 + lattice_dim)
        shifted = jnp.concatenate([inner_part, arrived], axis=2 + lattice_dim).reshape(
            6, site_count, vec_count
        )
        link_pair = links[lattice_dim]
        real_form = jnp.concatenate(
            [
                jnp.concatenate([link_pair[0], -link_pair[1]], axis=1),
                jnp.concatenate([link_pair[1], link_pair[0]], axis=1),
            ],
            axis=0,
        )
        product = jnp.einsum("ijs,jsn->isn", real_form, shifted, preferred_element_type=jnp.float32)
        displaced.append(product.astype(jnp.bfloat16).reshape(2, 3, site_count, vec_count))
    right_factor = jnp.stack(displaced, axis=3)
    swapped = jnp.concatenate([right_factor[1:2], -right_factor[0:1]], axis=0)
    combined = jnp.stack([right_factor, swapped], axis=3)
    extent = SIDE * blocks
    x_coord = positions[0] * SIDE + jnp.arange(SIDE, dtype=jnp.int32)
    y_coord = positions[1] * SIDE + jnp.arange(SIDE, dtype=jnp.int32)
    z_coord = positions[2] * SIDE + jnp.arange(SIDE, dtype=jnp.int32)
    phase_index = (
        momenta[:, 0, None, None, None] * x_coord[None, :, None, None]
        + momenta[:, 1, None, None, None] * y_coord[None, None, :, None]
        + momenta[:, 2, None, None, None] * z_coord[None, None, None, :]
    ) % extent
    angles = phase_index.reshape(momenta.shape[0], site_count).astype(jnp.float32) * (
        2.0 * math.pi / extent
    )
    cosine = jnp.cos(angles).T[None, :, :, None]
    sine_part = jnp.sin(angles).T[None, :, :, None]
    real_vec = vectors[0][:, :, None, :]
    imag_vec = vectors[1][:, :, None, :]
    left_factor = jnp.stack(
        [cosine * real_vec - sine_part * imag_vec, sine_part * real_vec + cosine * imag_vec]
    ).astype(jnp.bfloat16)
    row_count = vec_count // members
    summed = lax.psum(make_terms(left_factor, combined), "xyz")
    my_rows = lax.dynamic_slice_in_dim(summed, my_index * row_count, row_count, 0)
    selector = (directions[:, None] == jnp.arange(3, dtype=jnp.int32)[None, :]).astype(jnp.float32)
    normalise = 1.0 / math.sqrt(3.0 * site_count * members)
    result = (
        jnp.einsum("dk,aokmb->odmab", selector, my_rows, precision=lax.Precision.HIGHEST)
        * normalise
    )
    return result


def solution(mesh):
    in_specs = (P("ta", None, "xyz", None), P("ta", None, None, None, "xyz"), P(), P())
    out_specs = P("ta", None, None, "xyz", None)
    return jax.shard_map(
        per_device, mesh=mesh, in_specs=in_specs, out_specs=out_specs, check_vma=False
    )
```

profile of v0, /device:TPU:8, one launch (start us, length us, event | category | flops | bytes accessed | tf_op | source)
XLA Modules:
  0.0 244.2 jit_solution(15336477092447120177)
XLA Ops:
  6.5 1.6 slice.115
  8.1 8.8 %collective-permute-start.1 = (bf16[2,3,8,1,8,128]{5,4,3,2,1,0:T(8,128)(2,1)}, bf16[2,3,8,1,8,128]{5,4,3,2,1,0:T(8,128)(2,1)}, u32[]{:S(2)}, u32[]{:S(2)}) collective-permute-start(bf16[2,3,8,1,8,128]{5,4,3,2,1,0:T(8,128)(2,1)} %slice.115), channel_id=1, source_target_pairs={{0,52},{1,53},{2,54},{3,55},{4,56},{5,57},{6,58},{7,59},{8,60},{9,... | collective-permute-start | bytes 294920 | tf_op jit(solution)/shard_map/ppermute | solution.py:14
  17.0 1.2 slice.117
  18.7 5.6 %collective-permute-start.4 = (bf16[2,3,8,8,1,128]{5,4,3,2,1,0:T(2,128)(2,1)S(1)}, bf16[2,3,8,8,1,128]{5,4,3,2,1,0:T(2,128)(2,1)}, u32[]{:S(2)}, u32[]{:S(2)}) collective-permute-start(bf16[2,3,8,8,1,128]{5,4,3,2,1,0:T(2,128)(2,1)S(1)} %slice.117), channel_id=1, source_target_pairs={{0,63},{1,0},{2,1},{3,2},{4,3},{5,4},{6,5},{7,6},{8,7},{9,8},{10,9... | collective-permute-start | bytes 294920 | tf_op jit(solution)/shard_map/ppermute | solution.py:14
  24.3 1.5 slice.113
  26.1 2.0 slice.114
  28.1 1.2 slice.116
  29.2 0.9 slice.112
  30.2 1.0 bitcast_convert_fusion.1
  33.6 2.9 %subtract_convert_fusion = (bf16[1,3,512,2,128]{4,2,0,1,3:T(8,128)(2,1)}, bf16[1,3,512,2,128]{4,2,0,1,3:T(8,128)(2,1)}) fusion(f32[3,512,128]{2,1,0:T(8,128)} %get-tuple-element.23, f32[512,2]{0,1:T(2,128)S(1)} %sine_bitcast_fusion, f32[3,512,128]{2,1,0:T(8,128)S(1)} %get-tuple-element.22, f32[512,2]{0,1:T(2,128)S(1)} %get-tuple-element.8), kind=kLoop, calls=%fused_computation.16 | loop fusion | flops 3145728 | bytes 3153920 | tf_op jit(solution)/shard_map/convert.2
  37.3 0.9 broadcast_select_fusion.1
  38.2 1.2 pad_maximum_fusion.3
  39.4 0.8 fusion.13
  40.3 1.2 broadcast_select_fusion
  42.8 1.0 copy.50
  43.7 1.4 copy.57
  45.2 1.0 copy.55
  46.1 1.4 copy.58
  47.6 1.2 pad_maximum_fusion.2
  48.7 0.8 fusion.12
  50.7 0.9 copy-done.2
  53.6 1.0 pad_maximum_fusion.5
  54.6 180.2 %all-reduce.2.cloned.1.call-done = f32[128,2,3,2,128]{0,4,3,1,2:T(8,128)} async-done(((f32[128,2,3,2,128]{0,4,3,1,2:T(8,128)}), f32[128,2,3,2,128]{0,4,3,1,2:T(8,128)}) %all-reduce.2.cloned.1.call-update) | async-done | bytes 786448 | tf_op jit(solution)/shard_map/psum | solution.py:101
  234.8 1.4 constant_dynamic-slice_fusion
  (58 shorter events, 9.4 us)
Async XLA Ops:
  6.5 21.5 %copy-start = (bf16[2,3,512,128]{3,2,1,0:T(8,128)(2,1)S(1)}, bf16[2,3,512,128]{3,2,1,0:T(8,128)(2,1)}, u32[]{:S(2)}) copy-start(bf16[2,3,512,128]{3,2,1,0:T(8,128)(2,1)} %param.4) | copy-start | bytes 2359300
  6.5 228.3 %all-reduce.2.cloned.1.call-start = ((), (), s32[]{:S(2)}) async-start(), calls=%async_computation | async-start | bytes 1572864 | tf_op jit(solution)/shard_map/psum | solution.py:101
  8.1 29.1 %collective-permute-start.1 = (bf16[2,3,8,1,8,128]{5,4,3,2,1,0:T(8,128)(2,1)}, bf16[2,3,8,1,8,128]{5,4,3,2,1,0:T(8,128)(2,1)}, u32[]{:S(2)}, u32[]{:S(2)}) collective-permute-start(bf16[2,3,8,1,8,128]{5,4,3,2,1,0:T(8,128)(2,1)} %slice.115), channel_id=1, source_target_pairs={{0,52},{1,53},{2,54},{3,55},{4,56},{5,57},{6,58},{7,59},{8,60},{9,... | collective-permute-start | bytes 294920 | tf_op jit(solution)/shard_map/ppermute | solution.py:14
  16.9 20.4 %collective-permute-start.2 = (bf16[2,3,8,1,8,128]{5,4,3,2,1,0:T(8,128)(2,1)}, bf16[2,3,8,1,8,128]{5,4,3,2,1,0:T(8,128)(2,1)}, u32[]{:S(2)}, u32[]{:S(2)}) collective-permute-start(bf16[2,3,8,1,8,128]{5,4,3,2,1,0:T(8,128)(2,1)} %slice.115), channel_id=1, source_target_pairs={{0,4},{1,5},{2,6},{3,7},{4,8},{5,9},{6,10},{7,11},{8,12},{9,13},{1... | collective-permute-start | bytes 294920 | tf_op jit(solution)/shard_map/ppermute | solution.py:14
  18.2 22.0 %collective-permute-start.3 = (bf16[2,3,8,8,1,128]{5,4,3,2,1,0:T(2,128)(2,1)S(1)}, bf16[2,3,8,8,1,128]{5,4,3,2,1,0:T(2,128)(2,1)}, u32[]{:S(2)}, u32[]{:S(2)}) collective-permute-start(bf16[2,3,8,8,1,128]{5,4,3,2,1,0:T(2,128)(2,1)S(1)} %slice.117), channel_id=1, source_target_pairs={{0,3},{1,4},{2,5},{3,6},{4,7},{5,8},{6,9},{7,10},{8,11},{9,12},{10... | collective-permute-start | bytes 294920 | tf_op jit(solution)/shard_map/ppermute | solution.py:14
  18.7 21.6 %collective-permute-start.4 = (bf16[2,3,8,8,1,128]{5,4,3,2,1,0:T(2,128)(2,1)S(1)}, bf16[2,3,8,8,1,128]{5,4,3,2,1,0:T(2,128)(2,1)}, u32[]{:S(2)}, u32[]{:S(2)}) collective-permute-start(bf16[2,3,8,8,1,128]{5,4,3,2,1,0:T(2,128)(2,1)S(1)} %slice.117), channel_id=1, source_target_pairs={{0,63},{1,0},{2,1},{3,2},{4,3},{5,4},{6,5},{7,6},{8,7},{9,8},{10,9... | collective-permute-start | bytes 294920 | tf_op jit(solution)/shard_map/ppermute | solution.py:14
  25.8 21.7 %collective-permute-start = (bf16[2,3,1,8,8,128]{5,4,3,2,1,0:T(8,128)(2,1)}, bf16[2,3,1,8,8,128]{5,4,3,2,1,0:T(8,128)(2,1)S(1)}, u32[]{:S(2)}, u32[]{:S(2)}) collective-permute-start(bf16[2,3,1,8,8,128]{5,4,3,2,1,0:T(8,128)(2,1)} %slice.113), channel_id=1, source_target_pairs={{0,48},{1,49},{2,50},{3,51},{4,52},{5,53},{6,54},{7,55},{8,56},{9,... | collective-permute-start | bytes 294920 | tf_op jit(solution)/shard_map/ppermute | solution.py:14
  29.2 1.9 copy-start.4
  30.2 2.7 %copy-start.5 = (s32[2,3]{1,0:T(2,128)S(1)}, s32[2,3]{1,0:T(2,128)}, u32[]{:S(2)}) copy-start(s32[2,3]{1,0:T(2,128)} %param.6) | copy-start | bytes 76
  39.4 2.1 copy-start.1
  50.5 1.1 copy-start.2
  50.5 1.4 copy-start.3
  53.6 182.9 %copy-start.6 = (s32[3]{0:T(128)S(1)}, s32[3]{0:T(128)}, u32[]{:S(2)}) copy-start(s32[3]{0:T(128)} %param.7) | copy-start | bytes 40
Sparse Core Ops, SparseCore 0:
  54.7 180.0 all-reduce.1
where the time goes:
time: 245 us; the launch traced here: 244 us
  waiting for transfers between devices  180 us (73%)
  local copies, waits for them, and re-layouts  19.7 us (8%)
  starting transfers between devices  15.1 us (6%)
  between operations  13.7 us (6%)
  other arithmetic  11.1 us (5%)
  matrix products  4.39 us (2%)
    psum x1, waiting for transfers between devices, per_device(): summed = lax.psum(make_terms(left_factor, combined), 'xyz')  180 us
    ppermute x5, starting transfers between devices, passed_along(): return lax.ppermute(value, axis, pairs)  15.1 us
  transfers between devices with their start and end apart: 6, of which 1 were waited for; matrix products, arithmetic and copies ran while one was open for 10% of the time, Pallas kernels for 0%

commit v1 on v0

v1 whole, which is shorter than its diff:
```python
import functools
import math

import jax
import jax.numpy as jnp
from jax import lax
from jax.experimental import pallas as pl
from jax.experimental.pallas import tpu as pltpu
from jax.sharding import PartitionSpec as P

SIDE = 8
SITES = 512
FACE = 64
NVEC = 128
F32 = jnp.float32
BF16 = jnp.bfloat16
VMEM = pl.BlockSpec(memory_space=pltpu.VMEM)
SMEM = pl.BlockSpec(memory_space=pltpu.SMEM)
NT = (((1,), (1,)), ((), ()))


def face_site(face, direction, last):
    hi, lo = face >> 3, face & 7
    edge = SIDE - 1 if last else 0
    if direction == 0:
        return edge * 64 + face
    if direction == 1:
        return hi * 64 + edge * 8 + lo
    return face * 8 + edge


def layer_kernel(v_ref, x_ref, y_ref, z_ref):
    site = lax.broadcasted_iota(jnp.int32, (FACE, SITES), 1)
    face = lax.broadcasted_iota(jnp.int32, (FACE, SITES), 0)
    picks = [(site == face_site(face, d, False)).astype(BF16) for d in range(3)]
    pick = jnp.concatenate(picks, axis=0)
    for rc in range(6):
        layers = jnp.dot(pick, v_ref[rc], preferred_element_type=F32).astype(BF16)
        x_ref[rc] = layers[0:64]
        y_ref[rc] = layers[64:128]
        z_ref[rc] = layers[128:192]


def interior_kernel(mom_ref, v_ref, u_ref, part_ref, lf_ref, uf_ref, vt, lt, rt, ub, us):
    index = lax.axis_index("xyz")
    gx, gy, gz = index // 16, 3 - (index // 4) % 4, index % 4
    eye = (
        lax.broadcasted_iota(jnp.int32, (NVEC, NVEC), 0)
        == lax.broadcasted_iota(jnp.int32, (NVEC, NVEC), 1)
    ).astype(BF16)
    for rc in range(6):
        vt[rc] = lax.dot_general(eye, v_ref[rc], NT, preferred_element_type=F32)

    site = lax.broadcasted_iota(jnp.int32, (8, SITES), 1)
    lx, ly, lz = site >> 6, (site >> 3) & 7, site & 7
    phases = []
    for p in range(2):
        k = (
            mom_ref[p, 0] * (gx * 8 + lx)
            + mom_ref[p, 1] * (gy * 8 + ly)
            + mom_ref[p, 2] * (gz * 8 + lz)
        ) & 31
        angle = k.astype(F32) * (2.0 * math.pi / 32)
        phases.append((jnp.cos(angle)[None], jnp.sin(angle)[None]))

    inner = [(local < SIDE - 1).astype(F32) for local in (lx, ly, lz)]
    for d in range(3):
        for ij in range(9):
            pair = u_ref[d * 9 + ij].astype(F32)
            us[pl.ds((d * 9 + ij) * 2, 2), :] = pair
            for r in range(2):
                ub[d * 18 + ij * 2 + r] = pair[r : r + 1] * inner[d]
    us[pl.ds(54, 10), :] = jnp.zeros((10, SITES), F32)

    upper = lax.broadcasted_iota(jnp.int32, (1, 8, 128), 2) >= 64

    def rows_step(block, _):
        row = pl.multiple_of(block * 16, 16)
        rows = pl.ds(row, 16)
        for c in range(3):
            re = vt[c, rows, :].reshape(2, 8, SITES)
            im = vt[3 + c, rows, :].reshape(2, 8, SITES)
            for p in range(2):
                cosine, sine = phases[p]
                lanes = pl.ds(c * SITES, SITES)
                out = pl.ds(pl.multiple_of(p * 128 + row, 16), 16)
                lt[out, lanes] = (cosine * re - sine * im).reshape(16, SITES).astype(BF16)
                out = pl.ds(pl.multiple_of(256 + p * 128 + row, 16), 16)
                lt[out, lanes] = (sine * re + cosine * im).reshape(16, SITES).astype(BF16)
        for d in range(3):
            for k in range(4):
                lanes = pl.ds(k * 128, 128)
                shifted = []
                for rc in range(6):
                    here = vt[rc, rows, lanes]
                    if d == 2:
                        here = pltpu.roll(here, 127, 1)
                    elif d == 1:
                        here = pltpu.roll(here, 120, 1)
                    else:
                        here = pltpu.roll(here, 64, 1)
                        if k < 3:
                            after = pltpu.roll(vt[rc, rows, pl.ds(k * 128 + 128, 128)], 64, 1)
                            here = jnp.where(upper[0, 0:1], after, here)
                    shifted.append(here.reshape(2, 8, 128))
                for i in range(3):
                    dr = di = None
                    for j in range(3):
                        ur = ub[d * 18 + i * 6 + j * 2, :, lanes][None]
                        ui = ub[d * 18 + i * 6 + j * 2 + 1, :, lanes][None]
                        vr, vi = shifted[j], shifted[3 + j]
                        tr, ti = ur * vr - ui * vi, ui * vr + ur * vi
                        dr, di = (tr, ti) if dr is None else (dr + tr, di + ti)
                    lanes_out = pl.ds(i * SITES + k * 128, 128)
                    rt[d, rows, lanes_out] = dr.reshape(16, 128).astype(BF16)
                    out = pl.ds(pl.multiple_of(128 + row, 16), 16)
                    rt[d, out, lanes_out] = di.reshape(16, 128).astype(BF16)
        return 0

    lax.fori_loop(0, 8, rows_step, 0)

    for d in range(3):
        full = lax.dot_general(lt[...], rt[d], NT, preferred_element_type=F32)
        for p in range(2):
            re_rows, im_rows = full[p * 128 : p * 128 + 128], full[256 + p * 128 : 384 + p * 128]
            part_ref[d * 4 + p * 2] = re_rows[:, :128] + im_rows[:, 128:]
            part_ref[d * 4 + p * 2 + 1] = re_rows[:, 128:] - im_rows[:, :128]

    site_c = lax.broadcasted_iota(jnp.int32, (SITES, FACE), 0)
    face_c = lax.broadcasted_iota(jnp.int32, (SITES, FACE), 1)
    site_r = lax.broadcasted_iota(jnp.int32, (FACE, SITES), 1)
    face_r = lax.broadcasted_iota(jnp.int32, (FACE, SITES), 0)
    for d in range(3):
        pick_c = (site_c == face_site(face_c, d, True)).astype(BF16)
        pick_r = (site_r == face_site(face_r, d, True)).astype(BF16)
        for c in range(3):
            lf_ref[d, c] = jnp.dot(
                lt[:, c * SITES : (c + 1) * SITES], pick_c, preferred_element_type=F32
            ).astype(BF16)
        uf_ref[d] = lax.dot_general(pick_r, us[...].astype(BF16), NT, preferred_element_type=F32)


def boundary_kernel(part_ref, lf_ref, uf_ref, x_ref, y_ref, z_ref, send_ref, keep_ref, tile, chunk):
    core = lax.axis_index("xyz") % 2
    for d, layer_ref in enumerate((x_ref, y_ref, z_ref)):
        total = None
        layer = [layer_ref[rc].astype(F32) for rc in range(6)]
        for i in range(3):
            dr = di = None
            for j in range(3):
                q = d * 18 + i * 6 + j * 2
                ur = jnp.broadcast_to(uf_ref[d, :, q : q + 1], (FACE, NVEC))
                ui = jnp.broadcast_to(uf_ref[d, :, q + 1 : q + 2], (FACE, NVEC))
                vr, vi = layer[j], layer[3 + j]
                tr, ti = ur * vr - ui * vi, ui * vr + ur * vi
                dr, di = (tr, ti) if dr is None else (dr + tr, di + ti)
            right = jnp.concatenate([dr.astype(BF16), di.astype(BF16)], axis=1)
            term = jnp.dot(lf_ref[d, i], right, preferred_element_type=F32)
            total = term if total is None else total + term
        for p in range(2):
            re_rows, im_rows = total[p * 128 : p * 128 + 128], total[256 + p * 128 : 384 + p * 128]
            t = d * 4 + p * 2
            tile[t] = part_ref[t] + re_rows[:, :128] + im_rows[:, 128:]
            tile[t + 1] = part_ref[t + 1] + re_rows[:, 128:] - im_rows[:, :128]
    for which, parity in ((0, core), (1, 1 - core)):
        for t in range(12):
            for r in range(2):
                rows = tile[t, pl.ds(2 * parity + r, 32, stride=4), :]
                chunk[which, pl.ds(t * 2 + r, 32, stride=24), :] = rows
    keep_ref[...] = chunk[0]
    send_ref[...] = chunk[1].astype(BF16)


def final_kernel(scale, dir_ref, got_ref, out_ref, acc):
    acc[...] = jnp.sum(got_ref[...].astype(F32), axis=0) * scale
    for d in range(3):
        rows = acc[pl.ds(pl.multiple_of(dir_ref[d] * 8, 8), 8), :]
        for p in range(2):
            for o in range(2):
                t = (p * 2 + o) * 2
                out_ref[o, d, p] = rows[t : t + 2]


def shape(dims, dtype):
    return jax.ShapeDtypeStruct(dims, dtype)


def per_device(vectors, links, momenta, directions):
    params = pltpu.CompilerParams(vmem_limit_bytes=48 * 1024 * 1024)
    field = vectors.reshape(6, SITES, NVEC)
    rows = links.transpose(0, 2, 3, 1, 4).reshape(27, 2, SITES)
    face = shape((6, FACE, NVEC), BF16)
    layers = pl.pallas_call(
        layer_kernel,
        out_shape=[face] * 3,
        in_specs=[VMEM],
        out_specs=[VMEM] * 3,
        compiler_params=params,
    )(field)
    step_x = [(i, (i - 16) % 64) for i in range(64)]
    step_y = [(i, (i & ~12) | ((i + 4) & 12)) for i in range(64)]
    step_z = [(i, (i & ~3) | ((i - 1) & 3)) for i in range(64)]
    arrived = [lax.ppermute(a, "xyz", s) for a, s in zip(layers, (step_x, step_y, step_z))]
    part, left_face, link_face = pl.pallas_call(
        interior_kernel,
        out_shape=[
            shape((12, NVEC, NVEC), F32),
            shape((3, 3, 512, FACE), BF16),
            shape((3, FACE, 64), F32),
        ],
        in_specs=[SMEM, VMEM, VMEM],
        out_specs=[VMEM] * 3,
        scratch_shapes=[
            pltpu.VMEM((6, NVEC, SITES), F32),
            pltpu.VMEM((512, 3 * SITES), BF16),
            pltpu.VMEM((3, 256, 3 * SITES), BF16),
            pltpu.VMEM((54, 8, SITES), F32),
            pltpu.VMEM((64, SITES), F32),
        ],
        compiler_params=params,
        cost_estimate=pl.CostEstimate(
            flops=2_000_000_000, bytes_accessed=4_000_000, transcendentals=0
        ),
    )(momenta, field, rows)
    send, keep = pl.pallas_call(
        boundary_kernel,
        out_shape=[shape((768, NVEC), BF16), shape((768, NVEC), F32)],
        in_specs=[VMEM] * 6,
        out_specs=[VMEM] * 2,
        scratch_shapes=[pltpu.VMEM((12, NVEC, NVEC), F32), pltpu.VMEM((2, 768, NVEC), F32)],
        compiler_params=params,
    )(part, left_face, link_face, *arrived)
    other = lax.ppermute(send, "xyz", [(i, i ^ 1) for i in range(64)])
    chip = (keep + other.astype(F32)).astype(BF16).reshape(32, 24, NVEC)
    groups = [[2 * c + core for c in range(32)] for core in range(2)]
    got = lax.all_to_all(chip, "xyz", 0, 0, axis_index_groups=groups, tiled=True)
    return pl.pallas_call(
        functools.partial(final_kernel, 1.0 / math.sqrt(3.0 * SITES * 64)),
        out_shape=shape((2, 3, 2, 2, NVEC), F32),
        in_specs=[SMEM, VMEM],
        out_specs=VMEM,
        scratch_shapes=[pltpu.VMEM((24, NVEC), F32)],
        compiler_params=params,
    )(directions, got)


def solution(mesh):
    in_specs = (P("ta", None, "xyz", None), P("ta", None, None, None, "xyz"), P(), P())
    out_specs = P("ta", None, None, "xyz", None)
    return jax.shard_map(
        per_device, mesh=mesh, in_specs=in_specs, out_specs=out_specs, check_vma=False
    )
```

time: 245 us -> 40.7 us (0.17)
  waiting for transfers between devices: 180 us -> 1.08 us
  blocking collectives: 0 us -> 16.1 us
  local copies, waits for them, and re-layouts: 19.7 us -> 3.76 us
  between operations: 13.7 us -> 0.06 us
  other arithmetic: 11.1 us -> 0.05 us
  Pallas kernels: 0 us -> 9.35 us
  starting transfers between devices: 15.1 us -> 10 us
  matrix products: 4.39 us -> 0 us
    psum x1 -> x0, waiting for transfers between devices: 180 us -> none  [per_device(): summed = lax.psum(make_terms(left_factor, combined), 'xyz')]
    all_to_all x0 -> x1, blocking collectives: none -> 16.1 us  [per_device(): lax.all_to_all(chip, 'xyz', 0, 0, axis_index_groups=groups, tiled=True)]
    pallas_call x0 -> x4, Pallas kernels: none -> 9.35 us  [the longest x1 6.45 us: per_device(): pl.pallas_call(interior_kernel, out_shape=[shape((12, NVEC, NVEC), F32),...]
    slice x8 -> x0, local copies, waits for them, and re-layouts: 8.73 us -> none  [the longest x3 4.38 us: per_device(): boundary = lax.slice_in_dim(lattice_block, 0, 1, axis=2 + lattice_dim)]
    ppermute x5 -> x4, starting transfers between devices: 15.1 us -> 10 us  [the longest x3 9.41 us: per_device(): lax.ppermute(a, 'xyz', s)]
    another operation x4 -> x0, other arithmetic: 4.45 us -> none
    dot_general x7 -> x0, matrix products: 4.39 us -> none  [the longest x3 2.44 us: per_device(): jnp.einsum('ijs,jsn->isn', real_form, shifted, preferred_element_type=jnp...]
    another operation x3 -> x0, local copies, waits for them, and re-layouts: 3.09 us -> none  [per_device(): right_factor = jnp.stack(displaced, axis=3)]
  transfers between devices with their start and end apart: 6 -> 4, of which waited for: 1 -> 1; matrix products, arithmetic and copies ran while one was open for 10% -> 0% of each run, Pallas kernels for 0% -> 16%
where the time goes in v1:
time: 40.7 us; the launch traced here: 40.4 us
  blocking collectives  16.1 us (40%)
  starting transfers between devices  10 us (25%)
  Pallas kernels  9.35 us (23%)
  local copies, waits for them, and re-layouts  3.76 us (9%)
  waiting for transfers between devices  1.08 us (3%)
    all_to_all x1, blocking collectives, per_device(): lax.all_to_all(chip, 'xyz', 0, 0, axis_index_groups=groups, tiled=True)  16.1 us
    ppermute x3, starting transfers between devices, per_device(): lax.ppermute(a, 'xyz', s)  9.41 us
    pallas_call x1, Pallas kernels, per_device(): pl.pallas_call(interior_kernel, out_shape=[shape((12, NVEC, NVEC), F32),...  6.45 us
    unnamed x10, local copies, waits for them, and re-layouts  3.76 us
    pallas_call x1, Pallas kernels, per_device(): pl.pallas_call(boundary_kernel, out_shape=[shape((768, NVEC), BF16), shap...  1.27 us
    pallas_call x1, Pallas kernels, per_device(): pl.pallas_call(functools.partial(final_kernel, 1.0 / math.sqrt(3.0 * SITE...  1.18 us
    ppermute x1, waiting for transfers between devices, per_device(): other = lax.ppermute(send, 'xyz', [(i, i ^ 1) for i in range(64)])  1.07 us
  transfers between devices with their start and end apart: 4, of which 1 were waited for; matrix products, arithmetic and copies ran while one was open for 0% of the time, Pallas kernels for 16%

profile of v1, /device:TPU:8, one launch (start us, length us, event | category | flops | bytes accessed | tf_op | source)
XLA Modules:
  0.0 40.4 jit_solution(3463181325248779195)
XLA Ops:
  0.0 0.0 copy-start
  0.0 1.1 %copy-done = bf16[2,3,512,128]{3,2,1,0:T(8,128)(2,1)S(1)} copy-done((bf16[2,3,512,128]{3,2,1,0:T(8,128)(2,1)S(1)}, bf16[2,3,512,128]{3,2,1,0:T(8,128)(2,1)}, u32[]{:S(2)}) %copy-start) | copy-done | bytes 786456
  1.1 0.5 %shard_map.47 = (bf16[6,64,128]{2,1,0:T(8,128)(2,1)S(1)}, bf16[6,64,128]{2,1,0:T(8,128)(2,1)S(1)}, bf16[6,64,128]{2,1,0:T(8,128)(2,1)S(1)}) custom-call(bf16[6,512,128]{2,1,0:T(8,128)(2,1)S(1)} %bitcast.5), custom_call_target="tpu_custom_call" | custom-call | tf_op jit(solution)/shard_map/pallas_call | solution.py:193
  1.6 6.4 %collective-permute-start = (bf16[6,64,128]{2,1,0:T(8,128)(2,1)S(1)}, bf16[6,64,128]{2,1,0:T(8,128)(2,1)S(1)}, u32[]{:S(2)}, u32[]{:S(2)}) collective-permute-start(bf16[6,64,128]{2,1,0:T(8,128)(2,1)S(1)} %get-tuple-element.16), channel_id=1, source_target_pairs={{0,48},{1,49},{2,50},{3,51},{4,52},{5,53},{6,54},{7,55},{8,56},{9,... | collective-permute-start | bytes 294920 | tf_op jit(solution)/shard_map/ppermute | solution.py:203
  8.0 3.0 %collective-permute-start.1 = (bf16[6,64,128]{2,1,0:T(8,128)(2,1)S(1)}, bf16[6,64,128]{2,1,0:T(8,128)(2,1)S(1)}, u32[]{:S(2)}, u32[]{:S(2)}) collective-permute-start(bf16[6,64,128]{2,1,0:T(8,128)(2,1)S(1)} %get-tuple-element.17), channel_id=1, source_target_pairs={{0,4},{1,5},{2,6},{3,7},{4,8},{5,9},{6,10},{7,11},{8,12},{9,13},{1... | collective-permute-start | bytes 294920 | tf_op jit(solution)/shard_map/ppermute | solution.py:203
  11.0 0.0 collective-permute-start.2
  11.0 0.0 copy-start.1
  11.0 1.1 %copy-done.1 = bf16[2,3,512,128]{3,2,1,0:T(8,128)(2,1)S(1)} copy-done((bf16[2,3,512,128]{3,2,1,0:T(8,128)(2,1)S(1)}, bf16[2,3,512,128]{3,2,1,0:T(8,128)(2,1)}, u32[]{:S(2)}) %copy-start.1) | copy-done | bytes 786456
  12.1 0.0 copy-start.3
  12.1 0.8 %copy-done.3 = bf16[3,2,3,3,512]{4,1,3,2,0:T(2,128)(2,1)S(1)} copy-done((bf16[3,2,3,3,512]{4,1,3,2,0:T(2,128)(2,1)S(1)}, bf16[3,2,3,3,512]{4,1,3,2,0:T(2,128)(2,1)}, u32[]{:S(2)}) %copy-start.3) | copy-done | bytes 55320
  13.0 0.0 copy-start.4
  13.0 0.7 %copy-done.4 = s32[2,3]{1,0:T(2,128)S(1)} copy-done((s32[2,3]{1,0:T(2,128)S(1)}, s32[2,3]{1,0:T(2,128)}, u32[]{:S(2)}) %copy-start.4) | copy-done | bytes 48
  13.6 6.4 %shard_map.46 = (f32[12,128,128]{2,1,0:T(8,128)S(1)}, bf16[3,3,512,64]{3,2,1,0:T(8,128)(2,1)S(1)}, f32[3,64,64]{2,1,0:T(8,128)S(1)}) custom-call(s32[2,3]{1,0:T(2,128)S(1)} %copy-done.4, bf16[6,512,128]{2,1,0:T(8,128)(2,1)S(1)} %bitcast.6, bf16[27,2,512]{2,1,0:T(2,128)(2,1)S(1)} %bitcast.7), custom_call_target="tpu_custom_call" | custom-call | flops 2000000000 | bytes 4000000 | tf_op jit(solution)/shard_map/pallas_call | solution.py:204
  20.1 0.0 collective-permute-done.x_ref
  20.1 0.0 collective-permute-done.1.y_ref
  20.1 0.0 collective-permute-done.2.z_ref
  20.1 1.3 %shard_map.48 = (bf16[768,128]{1,0:T(8,128)(2,1)S(1)}, f32[768,128]{1,0:T(8,128)S(1)}) custom-call(f32[12,128,128]{2,1,0:T(8,128)S(1)} %get-tuple-element.13.part_ref, bf16[3,3,512,64]{3,2,1,0:T(8,128)(2,1)S(1)} %get-tuple-element.14.lf_ref, f32[3,64,64]{2,1,0:T(8,128)S(1)} %get-tuple-element.15.uf_ref, bf16[6,64,128]{2,1,0:T(8,128)(2,1)S(1)} %collective-permute-done.x_ref, ...), custom_call_target="tpu_custom_call" | custom-call | tf_op jit(solution)/shard_map/pallas_call | solution.py:225
  21.4 0.0 copy-start.2
  21.4 0.6 %collective-permute-start.3 = (bf16[768,128]{1,0:T(8,128)(2,1)S(1)}, bf16[768,128]{1,0:T(8,128)(2,1)S(1)}, u32[]{:S(2)}, u32[]{:S(2)}) collective-permute-start(bf16[768,128]{1,0:T(8,128)(2,1)S(1)} %get-tuple-element.20), channel_id=1, source_target_pairs={{0,1},{1,0},{2,3},{3,2},{4,5},{5,4},{6,7},{7,6},{8,9},{9,8},{10,11... | collective-permute-start | bytes 589832 | tf_op jit(solution)/shard_map/ppermute | solution.py:233
  22.0 1.1 %collective-permute-done.3 = bf16[768,128]{1,0:T(8,128)(2,1)S(1)} collective-permute-done((bf16[768,128]{1,0:T(8,128)(2,1)S(1)}, bf16[768,128]{1,0:T(8,128)(2,1)S(1)}, u32[]{:S(2)}, u32[]{:S(2)}) %collective-permute-start.3) | collective-permute-done | bytes 196640 | tf_op jit(solution)/shard_map/ppermute | solution.py:233
  23.1 0.1 add_convert_fusion
  23.1 16.1 %all_to_all.5.got_ref = bf16[32,24,128]{2,1,0:T(8,128)(2,1)S(1)} all-to-all(bf16[32,24,128]{2,1,0:T(8,128)(2,1)S(1)} %bitcast.8), channel_id=1, replica_groups={{0,2,4,6,8,10,12,14,16,18,20,22,24,26,28,30,32,34,36,38,40,42,44,46,48,..., dimensions={0} | all-to-all | bytes 393216 | tf_op jit(solution)/shard_map/all_to_all | solution.py:236
  39.2 0.0 copy-done.2
  39.2 1.2 %shard_map.49 = f32[2,3,2,2,128]{4,3,2,1,0:T(2,128)} custom-call(s32[3]{0:T(128)S(1)} %copy-done.2, bf16[32,24,128]{2,1,0:T(8,128)(2,1)S(1)} %all_to_all.5.got_ref), custom_call_target="tpu_custom_call" | custom-call | tf_op jit(solution)/shard_map/pallas_call | solution.py:237
Async XLA Ops:
  0.0 1.1 %copy-start = (bf16[2,3,512,128]{3,2,1,0:T(8,128)(2,1)S(1)}, bf16[2,3,512,128]{3,2,1,0:T(8,128)(2,1)}, u32[]{:S(2)}) copy-start(bf16[2,3,512,128]{3,2,1,0:T(8,128)(2,1)} %param.4) | copy-start | bytes 2359300
  1.6 18.5 %collective-permute-start = (bf16[6,64,128]{2,1,0:T(8,128)(2,1)S(1)}, bf16[6,64,128]{2,1,0:T(8,128)(2,1)S(1)}, u32[]{:S(2)}, u32[]{:S(2)}) collective-permute-start(bf16[6,64,128]{2,1,0:T(8,128)(2,1)S(1)} %get-tuple-element.16), channel_id=1, source_target_pairs={{0,48},{1,49},{2,50},{3,51},{4,52},{5,53},{6,54},{7,55},{8,56},{9,... | collective-permute-start | bytes 294920 | tf_op jit(solution)/shard_map/ppermute | solution.py:203
  8.0 12.1 %collective-permute-start.1 = (bf16[6,64,128]{2,1,0:T(8,128)(2,1)S(1)}, bf16[6,64,128]{2,1,0:T(8,128)(2,1)S(1)}, u32[]{:S(2)}, u32[]{:S(2)}) collective-permute-start(bf16[6,64,128]{2,1,0:T(8,128)(2,1)S(1)} %get-tuple-element.17), channel_id=1, source_target_pairs={{0,4},{1,5},{2,6},{3,7},{4,8},{5,9},{6,10},{7,11},{8,12},{9,13},{1... | collective-permute-start | bytes 294920 | tf_op jit(solution)/shard_map/ppermute | solution.py:203
  11.0 9.1 %collective-permute-start.2 = (bf16[6,64,128]{2,1,0:T(8,128)(2,1)S(1)}, bf16[6,64,128]{2,1,0:T(8,128)(2,1)S(1)}, u32[]{:S(2)}, u32[]{:S(2)}) collective-permute-start(bf16[6,64,128]{2,1,0:T(8,128)(2,1)S(1)} %get-tuple-element.18), channel_id=1, source_target_pairs={{0,3},{1,0},{2,1},{3,2},{4,7},{5,4},{6,5},{7,6},{8,11},{9,8},{10,9... | collective-permute-start | bytes 294920 | tf_op jit(solution)/shard_map/ppermute | solution.py:203
  11.0 1.1 %copy-start.1 = (bf16[2,3,512,128]{3,2,1,0:T(8,128)(2,1)S(1)}, bf16[2,3,512,128]{3,2,1,0:T(8,128)(2,1)}, u32[]{:S(2)}) copy-start(bf16[2,3,512,128]{3,2,1,0:T(8,128)(2,1)} %param.4) | copy-start | bytes 2359300
  12.1 0.8 %copy-start.3 = (bf16[3,2,3,3,512]{4,1,3,2,0:T(2,128)(2,1)S(1)}, bf16[3,2,3,3,512]{4,1,3,2,0:T(2,128)(2,1)}, u32[]{:S(2)}) copy-start(bf16[3,2,3,3,512]{4,1,3,2,0:T(2,128)(2,1)} %param.5) | copy-start | bytes 165892
  13.0 0.7 %copy-start.4 = (s32[2,3]{1,0:T(2,128)S(1)}, s32[2,3]{1,0:T(2,128)}, u32[]{:S(2)}) copy-start(s32[2,3]{1,0:T(2,128)} %mom_ref.1) | copy-start | bytes 76
  21.4 17.8 %copy-start.2 = (s32[3]{0:T(128)S(1)}, s32[3]{0:T(128)}, u32[]{:S(2)}) copy-start(s32[3]{0:T(128)} %dir_ref.1) | copy-start | bytes 40
  21.4 1.7 %collective-permute-start.3 = (bf16[768,128]{1,0:T(8,128)(2,1)S(1)}, bf16[768,128]{1,0:T(8,128)(2,1)S(1)}, u32[]{:S(2)}, u32[]{:S(2)}) collective-permute-start(bf16[768,128]{1,0:T(8,128)(2,1)S(1)} %get-tuple-element.20), channel_id=1, source_target_pairs={{0,1},{1,0},{2,3},{3,2},{4,5},{5,4},{6,7},{7,6},{8,9},{9,8},{10,11... | collective-permute-start | bytes 589832 | tf_op jit(solution)/shard_map/ppermute | solution.py:233

commit v2 on v1

v2 whole, which is shorter than its diff:
```python
import functools
import math

import jax
import jax.numpy as jnp
from jax import lax
from jax.experimental import pallas as pl
from jax.experimental.pallas import tpu as pltpu
from jax.sharding import PartitionSpec as P

SIDE = 8
SITES = 512
FACE = 64
NVEC = 128
F32 = jnp.float32
BF16 = jnp.bfloat16
VMEM = pl.BlockSpec(memory_space=pltpu.VMEM)
HBM = pl.BlockSpec(memory_space=pltpu.HBM)
NT = (((1,), (1,)), ((), ()))


def iota(dims, axis):
    return lax.broadcasted_iota(jnp.int32, dims, axis)


def face_site(face, direction):
    hi, lo = face >> 3, face & 7
    return ((SIDE - 1) * 64 + face, hi * 64 + (SIDE - 1) * 8 + lo, face * 8 + SIDE - 1)[direction]


def layers(ref, index, layer):
    yield ref[index, pl.ds(layer * 64, 64), :]
    yield jnp.concatenate([ref[index, pl.ds(n * 64 + layer * 8, 8), :] for n in range(8)], axis=0)
    yield ref[index, pl.ds(layer, 64, stride=8), :]


def layer_kernel(v_ref, held_ref, x_ref, y_ref, z_ref, wide):
    for rc in range(6):
        wide[rc] = v_ref[rc].astype(F32)
        for out_ref, rows in zip((x_ref, y_ref, z_ref), layers(wide, rc, 0)):
            out_ref[rc] = rows.astype(BF16)


def link_product(link, shifted):
    for i in range(3):
        dr = di = None
        for j in range(3):
            ur, ui = link(i, j)
            vr, vi = shifted[j], shifted[3 + j]
            tr, ti = ur * vr - ui * vi, ui * vr + ur * vi
            dr, di = (tr, ti) if dr is None else (dr + tr, di + ti)
        yield i, dr, di


def complex_parts(full):
    top, bottom = full[:128], full[128:]
    return top[:, :128] + bottom[:, 128:], top[:, 128:] - bottom[:, :128]


def interior_kernel(
    mom_hbm, u, v_ref, part0_ref, part1_ref, lf0_ref, lf1_ref, uf_ref,
    mom, sem, wide, vt, vo, vl, lt, rt, ub, us, ut,
):
    copy = pltpu.make_async_copy(mom_hbm, mom, sem)
    copy.start()
    index = lax.axis_index("xyz")
    gx, gy, gz, core = index // 16, 3 - (index // 4) % 4, index % 4, index % 2

    row, column = iota((256, NVEC), 0), iota((256, NVEC), 1)
    whose = jnp.where(row < 128, 1 - core, core)
    order = (column == 4 * ((row >> 2) & 31) + 2 * whose + (row & 1)).astype(BF16)
    plain = (iota((NVEC, NVEC), 0) == iota((NVEC, NVEC), 1)).astype(BF16)
    both = jnp.concatenate([plain, order], axis=0)
    for rc in range(6):
        turned = lax.dot_general(both, v_ref[rc], NT, preferred_element_type=F32)
        for k in range(4):
            vt[rc, k] = turned[:128, k * 128 : k * 128 + 128]
        vo[rc] = turned[128:]
        wide[rc] = v_ref[rc].astype(F32)
        last = jnp.concatenate(list(layers(wide, rc, SIDE - 1)), axis=0).astype(BF16)
        turned = lax.dot_general(order, last, NT, preferred_element_type=F32)
        for d in range(3):
            place = pl.ds((rc % 3) * FACE, FACE)
            vl[d * 2 + rc // 3, :, place] = turned[:, d * FACE : d * FACE + FACE]
    copy.wait()

    def phase(site):
        lx, ly, lz = site >> 6, (site >> 3) & 7, site & 7
        second = ((iota(site.shape, 0) >> 1) & 1) == 1
        m = [jnp.where(second, mom[1, axis], mom[0, axis]) for axis in range(3)]
        k = (m[0] * (gx * 8 + lx) + m[1] * (gy * 8 + ly) + m[2] * (gz * 8 + lz)) & 31
        angle = k.astype(F32) * (2.0 * math.pi / 32)
        return jnp.cos(angle)[None], jnp.sin(angle)[None]

    def rotate(re, im, turn, width):
        cosine, sine = turn
        re, im = re.reshape(-1, 8, width), im.reshape(-1, 8, width)
        left = (cosine * re - sine * im).reshape(-1, width).astype(BF16)
        return left, (sine * re + cosine * im).reshape(-1, width).astype(BF16)

    site = iota((8, SITES), 1)
    turn = phase(site)
    for block in range(16):
        rows = pl.ds(block * 16, 16)
        for c in range(3):
            left = rotate(vo[c, rows, :], vo[3 + c, rows, :], turn, SITES)
            for ri in range(2):
                out = pl.ds((block // 8) * 256 + ri * 128 + (block % 8) * 16, 16)
                lt[out, pl.ds(c * SITES, SITES)] = left[ri]
    for d in range(3):
        turn = phase(face_site(iota((8, 3 * FACE), 1) & 63, d))
        left = rotate(vl[d * 2], vl[d * 2 + 1], turn, 3 * FACE)
        for ri in range(2):
            lf0_ref[d, pl.ds(ri * 128, 128), :] = left[ri][:128]
            lf1_ref[d, pl.ds(ri * 128, 128), :] = left[ri][128:]

    inner = [(n < SIDE - 1).astype(F32) for n in (site >> 6, (site >> 3) & 7, site & 7)]
    us[pl.ds(54, 74), :] = jnp.zeros((74, SITES), F32)
    for d in range(3):
        for ij in range(9):
            pair = u[d * 9 + ij].astype(F32)
            us[pl.ds((d * 9 + ij) * 2, 2), :] = pair
            for r in range(2):
                ub[d * 18 + ij * 2 + r] = pair[r : r + 1] * inner[d]
    for k in range(4):
        ut[0, pl.ds(k * 128, 128), :] = us[:, k * 128 : k * 128 + 128].T
    for d, rows in enumerate(layers(ut, 0, SIDE - 1)):
        uf_ref[d] = rows

    upper = iota((16, 128), 1) >= 64
    for d in range(3):
        for block in range(8):
            rows = pl.ds(block * 16, 16)
            for k in range(4):
                lanes = pl.ds(k * 128, 128)
                shifted = []
                for rc in range(6):
                    here = pltpu.roll(vt[rc, k, rows, :], (64, 120, 127)[d], 1)
                    if d == 0 and k < 3:
                        after = pltpu.roll(vt[rc, k + 1, rows, :], 64, 1)
                        here = jnp.where(upper, after, here)
                    shifted.append(here.reshape(2, 8, 128))

                def link(i, j):
                    q = d * 18 + i * 6 + j * 2
                    return ub[q, :, lanes][None], ub[q + 1, :, lanes][None]

                for i, dr, di in link_product(link, shifted):
                    lanes_out = pl.ds(i * SITES + k * 128, 128)
                    rt[d, rows, lanes_out] = dr.reshape(16, 128).astype(BF16)
                    rt[d, pl.ds(128 + block * 16, 16), lanes_out] = di.reshape(16, 128).astype(BF16)
    for d in range(3):
        full = lax.dot_general(lt[...], rt[d], NT, preferred_element_type=F32)
        for half, out_ref in enumerate((part0_ref, part1_ref)):
            re, im = complex_parts(full[half * 256 : half * 256 + 256])
            out_ref[d * 2] = re
            out_ref[d * 2 + 1] = im


def boundary_half(part_ref, lf_ref, right, chunk):
    low = iota((16, 8, NVEC), 1) < 4
    for d in range(3):
        term = jnp.dot(lf_ref[d], right(d), preferred_element_type=F32)
        re, im = complex_parts(term)
        re = (part_ref[d * 2] + re).reshape(16, 8, NVEC)
        im = (part_ref[d * 2 + 1] + im).reshape(16, 8, NVEC)
        even = jnp.where(low, re, pltpu.roll(im, 4, 1))
        odd = jnp.where(low, pltpu.roll(re, 4, 1), im)
        pairs = jnp.stack([even, odd], axis=1).reshape(32, 8, NVEC)
        chunk[:, pl.ds(d * 8, 8), :] = pairs


def send_kernel(part_ref, lf_ref, uf_ref, x_ref, y_ref, z_ref, send_ref, right_ref, chunk):
    for d, layer_ref in enumerate((x_ref, y_ref, z_ref)):
        layer = [layer_ref[rc].astype(F32) for rc in range(6)]

        def link(i, j):
            q = d * 18 + i * 6 + j * 2
            return (
                jnp.broadcast_to(uf_ref[d, :, q : q + 1], (FACE, NVEC)),
                jnp.broadcast_to(uf_ref[d, :, q + 1 : q + 2], (FACE, NVEC)),
            )

        for i, dr, di in link_product(link, layer):
            right_ref[d, pl.ds(i * FACE, FACE), pl.ds(0, NVEC)] = dr.astype(BF16)
            right_ref[d, pl.ds(i * FACE, FACE), pl.ds(NVEC, NVEC)] = di.astype(BF16)
    boundary_half(part_ref, lf_ref, lambda d: right_ref[d], chunk)
    send_ref[...] = chunk[...].reshape(768, NVEC).astype(BF16)


def keep_kernel(dir_hbm, part_ref, lf_ref, right_ref, keep_ref, asked_ref, dirs, sem, chunk):
    copy = pltpu.make_async_copy(dir_hbm, dirs, sem)
    copy.start()
    boundary_half(part_ref, lf_ref, lambda d: right_ref[d], chunk)
    keep_ref[...] = chunk[...].reshape(768, NVEC)
    copy.wait()
    for slot in range(3):
        asked_ref[slot] = jnp.full((8, NVEC), dirs[slot], jnp.int32)


def final_kernel(scale, asked_ref, got_ref, out_ref):
    rows = jnp.sum(got_ref[...].astype(F32), axis=0) * scale
    for slot in range(3):
        chosen = jnp.where(asked_ref[slot] == 1, rows[8:16], rows[0:8])
        chosen = jnp.where(asked_ref[slot] == 2, rows[16:24], chosen)
        for o in range(2):
            for p in range(2):
                t = o * 4 + p * 2
                out_ref[o, slot, p] = chosen[t : t + 2]


def shape(dims, dtype):
    return jax.ShapeDtypeStruct(dims, dtype)


def per_device(vectors, links, momenta, directions):
    params = pltpu.CompilerParams(vmem_limit_bytes=48 * 1024 * 1024)
    field = vectors.reshape(6, SITES, NVEC)
    rows = links.transpose(0, 2, 3, 1, 4).reshape(27, 2, SITES)
    face = shape((6, FACE, NVEC), BF16)
    held, *first = pl.pallas_call(
        layer_kernel,
        out_shape=[shape((6, SITES, NVEC), BF16)] + [face] * 3,
        in_specs=[VMEM],
        out_specs=[VMEM] * 4,
        scratch_shapes=[pltpu.VMEM((6, SITES, NVEC), F32)],
        input_output_aliases={0: 0},
        compiler_params=params,
    )(field)
    step_x = [(i, (i - 16) % 64) for i in range(64)]
    step_y = [(i, (i & ~12) | ((i + 4) & 12)) for i in range(64)]
    step_z = [(i, (i & ~3) | ((i - 1) & 3)) for i in range(64)]
    arrived = [lax.ppermute(a, "xyz", s) for a, s in zip(first, (step_x, step_y, step_z))]
    part = shape((6, NVEC, NVEC), F32)
    left = shape((3, 256, 3 * FACE), BF16)
    part0, part1, left0, left1, link_face = pl.pallas_call(
        interior_kernel,
        out_shape=[part, part, left, left, shape((3, FACE, NVEC), F32)],
        in_specs=[HBM] + [VMEM] * 2,
        out_specs=[VMEM] * 5,
        scratch_shapes=[
            pltpu.SMEM((2, 3), jnp.int32),
            pltpu.SemaphoreType.DMA,
            pltpu.VMEM((6, SITES, NVEC), F32),
            pltpu.VMEM((6, 4, NVEC, 128), F32),
            pltpu.VMEM((6, 256, SITES), F32),
            pltpu.VMEM((6, 256, 3 * FACE), F32),
            pltpu.VMEM((512, 3 * SITES), BF16),
            pltpu.VMEM((3, 256, 3 * SITES), BF16),
            pltpu.VMEM((54, 8, SITES), F32),
            pltpu.VMEM((128, SITES), F32),
            pltpu.VMEM((1, SITES, 128), F32),
        ],
        compiler_params=params,
        cost_estimate=pl.CostEstimate(
            flops=2_000_000_000, bytes_accessed=4_000_000, transcendentals=0
        ),
    )(pltpu.with_memory_space_constraint(momenta, pltpu.HBM), rows, held)
    send, right = pl.pallas_call(
        send_kernel,
        out_shape=[shape((768, NVEC), BF16), shape((3, 3 * FACE, 256), BF16)],
        in_specs=[VMEM] * 6,
        out_specs=[VMEM] * 2,
        scratch_shapes=[pltpu.VMEM((32, 24, NVEC), F32)],
        compiler_params=params,
    )(part0, left0, link_face, *arrived)
    other = lax.ppermute(send, "xyz", [(i, i ^ 1) for i in range(64)])
    keep, asked = pl.pallas_call(
        keep_kernel,
        out_shape=[shape((768, NVEC), F32), shape((3, 8, NVEC), jnp.int32)],
        in_specs=[HBM] + [VMEM] * 3,
        out_specs=[VMEM] * 2,
        scratch_shapes=[
            pltpu.SMEM((3,), jnp.int32),
            pltpu.SemaphoreType.DMA,
            pltpu.VMEM((32, 24, NVEC), F32),
        ],
        compiler_params=params,
    )(pltpu.with_memory_space_constraint(directions, pltpu.HBM), part1, left1, right)
    chip = (keep + other.astype(F32)).astype(BF16).reshape(32, 24, NVEC)
    groups = [[2 * c + core for c in range(32)] for core in range(2)]
    got = lax.all_to_all(chip, "xyz", 0, 0, axis_index_groups=groups, tiled=True)
    return pl.pallas_call(
        functools.partial(final_kernel, 1.0 / math.sqrt(3.0 * SITES * 64)),
        out_shape=shape((2, 3, 2, 2, NVEC), F32),
        in_specs=[VMEM] * 2,
        out_specs=VMEM,
        compiler_params=params,
    )(asked, got)


def solution(mesh):
    in_specs = (P("ta", None, "xyz", None), P("ta", None, None, None, "xyz"), P(), P())
    out_specs = P("ta", None, None, "xyz", None)
    return jax.shard_map(
        per_device, mesh=mesh, in_specs=in_specs, out_specs=out_specs, check_vma=False
    )
```

time: 40.7 us -> 36.1 us (0.89)
  local copies, waits for them, and re-layouts: 3.76 us -> 1.14 us
  Pallas kernels: 9.35 us -> 8 us
  waiting for transfers between devices: 1.08 us -> 0.38 us
    unnamed x10 -> x3, local copies, waits for them, and re-layouts: 3.76 us -> 1.14 us
    pallas_call x3 -> x4, Pallas kernels: 8.17 us -> 7.36 us  [the longest x1 5.6 us: per_device(): pl.pallas_call(interior_kernel, out_shape=[part, part, left, left, shape(...]
    ppermute x1, waiting for transfers between devices: 1.07 us -> 0.37 us  [per_device(): other = lax.ppermute(send, 'xyz', [(i, i ^ 1) for i in range(64)])]
    pallas_call x1, Pallas kernels: 1.18 us -> 0.64 us  [per_device(): pl.pallas_call(functools.partial(final_kernel, 1.0 / math.sqrt(3.0 * SITE...]
  transfers between devices with their start and end apart: 4 -> 4, of which waited for: 1 -> 1; matrix products, arithmetic and copies ran while one was open for 0% -> 0% of each run, Pallas kernels for 16% -> 18%
where the time goes in v2:
time: 36.1 us; the launch traced here: 35.9 us
  blocking collectives  16.3 us (45%)
  starting transfers between devices  10 us (28%)
  Pallas kernels  8 us (22%)
  local copies, waits for them, and re-layouts  1.14 us (3%)
  waiting for transfers between devices  0.38 us (1%)
    all_to_all x1, blocking collectives, per_device(): lax.all_to_all(chip, 'xyz', 0, 0, axis_index_groups=groups, tiled=True)  16.3 us
    ppermute x3, starting transfers between devices, per_device(): lax.ppermute(a, 'xyz', s)  9.4 us
    pallas_call x1, Pallas kernels, per_device(): pl.pallas_call(interior_kernel, out_shape=[part, part, left, left, shape(...  5.6 us
    unnamed x3, local copies, waits for them, and re-layouts  1.14 us
    pallas_call x1, Pallas kernels, per_device(): pl.pallas_call(send_kernel, out_shape=[shape((768, NVEC), BF16), shape((3...  0.9 us
  transfers between devices with their start and end apart: 4, of which 1 were waited for; matrix products, arithmetic and copies ran while one was open for 0% of the time, Pallas kernels for 18%

profile of v2, /device:TPU:8, one launch (start us, length us, event | category | flops | bytes accessed | tf_op | source)
XLA Modules:
  0.0 35.9 jit_solution(475549121143599477)
XLA Ops:
  0.0 1.1 %copy.8 = bf16[2,3,512,128]{3,2,1,0:T(8,128)(2,1)S(1)} copy(bf16[2,3,512,128]{3,2,1,0:T(8,128)(2,1)} %param.4) | data formatting | bytes 1572864
  1.1 0.0 copy-start
  1.1 0.2 shard_map.46
  1.3 6.4 %collective-permute-start = (bf16[6,64,128]{2,1,0:T(8,128)(2,1)S(1)}, bf16[6,64,128]{2,1,0:T(8,128)(2,1)S(1)}, u32[]{:S(2)}, u32[]{:S(2)}) collective-permute-start(bf16[6,64,128]{2,1,0:T(8,128)(2,1)S(1)} %get-tuple-element.24), channel_id=1, source_target_pairs={{0,48},{1,49},{2,50},{3,51},{4,52},{5,53},{6,54},{7,55},{8,56},{9,... | collective-permute-start | bytes 294920 | tf_op jit(solution)/shard_map/ppermute | solution.py:233
  7.7 3.0 %collective-permute-start.1 = (bf16[6,64,128]{2,1,0:T(8,128)(2,1)S(1)}, bf16[6,64,128]{2,1,0:T(8,128)(2,1)S(1)}, u32[]{:S(2)}, u32[]{:S(2)}) collective-permute-start(bf16[6,64,128]{2,1,0:T(8,128)(2,1)S(1)} %get-tuple-element.25), channel_id=1, source_target_pairs={{0,4},{1,5},{2,6},{3,7},{4,8},{5,9},{6,10},{7,11},{8,12},{9,13},{1... | collective-permute-start | bytes 294920 | tf_op jit(solution)/shard_map/ppermute | solution.py:233
  10.7 0.0 collective-permute-start.2
  10.7 0.0 copy-done
  10.7 5.6 %shard_map.47 = (f32[6,128,128]{2,1,0:T(8,128)S(1)}, f32[6,128,128]{2,1,0:T(8,128)S(1)}, bf16[3,256,192]{2,1,0:T(8,128)(2,1)S(1)}, bf16[3,256,192]{2,1,0:T(8,128)(2,1)S(1)}, f32[3,64,128]{2,1,0:T(8,128)S(1)}) custom-call(s32[2,3]{1,0:T(2,128)} %mom_hbm.1, bf16[27,2,512]{2,1,0:T(2,128)(2,1)S(1)} %bitcast.6, bf16[6,512,128]{2,1,0:T(8,128)(2,1)S(1)} %get-tuple-element.18.v_ref), custom_call_target="tpu_custom_call" | custom-call | flops 2000000000 | bytes 4000000 | tf_op jit(solution)/shard_map/pallas_call | solution.py:236
  16.3 0.0 collective-permute-done.x_ref
  16.3 0.0 collective-permute-done.1.y_ref
  16.3 0.0 collective-permute-done.2.z_ref
  16.4 0.9 %shard_map.48 = (bf16[768,128]{1,0:T(8,128)(2,1)S(1)}, bf16[3,192,256]{2,1,0:T(8,128)(2,1)S(1)}) custom-call(f32[6,128,128]{2,1,0:T(8,128)S(1)} %get-tuple-element.21.part_ref, bf16[3,256,192]{2,1,0:T(8,128)(2,1)S(1)} %get-tuple-element.22.lf_ref, f32[3,64,128]{2,1,0:T(8,128)S(1)} %get-tuple-element.23.uf_ref, ...), custom_call_target="tpu_custom_call" | custom-call | tf_op jit(solution)/shard_map/pallas_call | solution.py:259
  17.3 0.6 %collective-permute-start.3 = (bf16[768,128]{1,0:T(8,128)(2,1)S(1)}, bf16[768,128]{1,0:T(8,128)(2,1)S(1)}, u32[]{:S(2)}, u32[]{:S(2)}) collective-permute-start(bf16[768,128]{1,0:T(8,128)(2,1)S(1)} %get-tuple-element.30), channel_id=1, source_target_pairs={{0,1},{1,0},{2,3},{3,2},{4,5},{5,4},{6,7},{7,6},{8,9},{9,8},{10,11... | collective-permute-start | bytes 589832 | tf_op jit(solution)/shard_map/ppermute | solution.py:267
  17.9 0.7 %shard_map.49 = (f32[768,128]{1,0:T(8,128)S(1)}, s32[3,8,128]{2,1,0:T(8,128)S(1)}) custom-call(s32[3]{0:T(128)} %dir_hbm.1, f32[6,128,128]{2,1,0:T(8,128)S(1)} %get-tuple-element.19.part_ref, bf16[3,256,192]{2,1,0:T(8,128)(2,1)S(1)} %get-tuple-element.20.lf_ref, bf16[3,192,256]{2,1,0:T(8,128)(2,1)S(1)} %get-tuple-element.27.right_ref), custom_call_target="tpu_custom_call" | custom-call | tf_op jit(solution)/shard_map/pallas_call | solution.py:268
  18.6 0.4 %collective-permute-done.3 = bf16[768,128]{1,0:T(8,128)(2,1)S(1)} collective-permute-done((bf16[768,128]{1,0:T(8,128)(2,1)S(1)}, bf16[768,128]{1,0:T(8,128)(2,1)S(1)}, u32[]{:S(2)}, u32[]{:S(2)}) %collective-permute-start.3) | collective-permute-done | bytes 196640 | tf_op jit(solution)/shard_map/ppermute | solution.py:267
  18.9 0.1 add_convert_fusion
  19.0 16.3 %all_to_all.5.got_ref = bf16[32,24,128]{2,1,0:T(8,128)(2,1)S(1)} all-to-all(bf16[32,24,128]{2,1,0:T(8,128)(2,1)S(1)} %bitcast.7), channel_id=1, replica_groups={{0,2,4,6,8,10,12,14,16,18,20,22,24,26,28,30,32,34,36,38,40,42,44,46,48,..., dimensions={0} | all-to-all | bytes 393216 | tf_op jit(solution)/shard_map/all_to_all | solution.py:282
  35.3 0.6 %shard_map.50 = f32[2,3,2,2,128]{4,3,2,1,0:T(2,128)} custom-call(s32[3,8,128]{2,1,0:T(8,128)S(1)} %get-tuple-element.28.asked_ref, bf16[32,24,128]{2,1,0:T(8,128)(2,1)S(1)} %all_to_all.5.got_ref), custom_call_target="tpu_custom_call" | custom-call | tf_op jit(solution)/shard_map/pallas_call | solution.py:283
Async XLA Ops:
  1.1 9.6 %copy-start = (bf16[3,2,3,3,512]{4,1,3,2,0:T(2,128)(2,1)S(1)}, bf16[3,2,3,3,512]{4,1,3,2,0:T(2,128)(2,1)}, u32[]{:S(2)}) copy-start(bf16[3,2,3,3,512]{4,1,3,2,0:T(2,128)(2,1)} %param.5) | copy-start | bytes 165892
  1.3 15.0 %collective-permute-start = (bf16[6,64,128]{2,1,0:T(8,128)(2,1)S(1)}, bf16[6,64,128]{2,1,0:T(8,128)(2,1)S(1)}, u32[]{:S(2)}, u32[]{:S(2)}) collective-permute-start(bf16[6,64,128]{2,1,0:T(8,128)(2,1)S(1)} %get-tuple-element.24), channel_id=1, source_target_pairs={{0,48},{1,49},{2,50},{3,51},{4,52},{5,53},{6,54},{7,55},{8,56},{9,... | collective-permute-start | bytes 294920 | tf_op jit(solution)/shard_map/ppermute | solution.py:233
  7.7 8.7 %collective-permute-start.1 = (bf16[6,64,128]{2,1,0:T(8,128)(2,1)S(1)}, bf16[6,64,128]{2,1,0:T(8,128)(2,1)S(1)}, u32[]{:S(2)}, u32[]{:S(2)}) collective-permute-start(bf16[6,64,128]{2,1,0:T(8,128)(2,1)S(1)} %get-tuple-element.25), channel_id=1, source_target_pairs={{0,4},{1,5},{2,6},{3,7},{4,8},{5,9},{6,10},{7,11},{8,12},{9,13},{1... | collective-permute-start | bytes 294920 | tf_op jit(solution)/shard_map/ppermute | solution.py:233
  10.7 5.6 %collective-permute-start.2 = (bf16[6,64,128]{2,1,0:T(8,128)(2,1)S(1)}, bf16[6,64,128]{2,1,0:T(8,128)(2,1)S(1)}, u32[]{:S(2)}, u32[]{:S(2)}) collective-permute-start(bf16[6,64,128]{2,1,0:T(8,128)(2,1)S(1)} %get-tuple-element.26), channel_id=1, source_target_pairs={{0,3},{1,0},{2,1},{3,2},{4,7},{5,4},{6,5},{7,6},{8,11},{9,8},{10,9... | collective-permute-start | bytes 294920 | tf_op jit(solution)/shard_map/ppermute | solution.py:233
  17.3 1.7 %collective-permute-start.3 = (bf16[768,128]{1,0:T(8,128)(2,1)S(1)}, bf16[768,128]{1,0:T(8,128)(2,1)S(1)}, u32[]{:S(2)}, u32[]{:S(2)}) collective-permute-start(bf16[768,128]{1,0:T(8,128)(2,1)S(1)} %get-tuple-element.30), channel_id=1, source_target_pairs={{0,1},{1,0},{2,3},{3,2},{4,5},{5,4},{6,7},{7,6},{8,9},{9,8},{10,11... | collective-permute-start | bytes 589832 | tf_op jit(solution)/shard_map/ppermute | solution.py:267

commit v3 on v2

--- a/solution.py
+++ b/solution.py
@@ -34,7 +34,7 @@
     yield ref[index, pl.ds(layer, 64, stride=8), :]
 
 
-def layer_kernel(v_ref, held_ref, x_ref, y_ref, z_ref, wide):
+def layer_kernel(v_ref, held_ref, wide, x_ref, y_ref, z_ref):
     for rc in range(6):
         wide[rc] = v_ref[rc].astype(F32)
         for out_ref, rows in zip((x_ref, y_ref, z_ref), layers(wide, rc, 0)):
@@ -57,12 +57,16 @@
     return top[:, :128] + bottom[:, 128:], top[:, 128:] - bottom[:, :128]
 
 
-def interior_kernel(
-    mom_hbm, u, v_ref, part0_ref, part1_ref, lf0_ref, lf1_ref, uf_ref,
-    mom, sem, wide, vt, vo, vl, lt, rt, ub, us, ut,
+def factor_kernel(
+    mom_hbm, dir_hbm, u, v_ref, wide, vt, lt, ub, lf0_ref, lf1_ref, uf_ref, asked_ref,
+    mom, dirs, sems, vo, vl, us, ut,
 ):
-    copy = pltpu.make_async_copy(mom_hbm, mom, sem)
-    copy.start()
+    copies = [
+        pltpu.make_async_copy(mom_hbm, mom, sems.at[0]),
+        pltpu.make_async_copy(dir_hbm, dirs, sems.at[1]),
+    ]
+    for copy in copies:
+        copy.start()
     index = lax.axis_index("xyz")
     gx, gy, gz, core = index // 16, 3 - (index // 4) % 4, index % 4, index % 2
 
@@ -71,18 +75,21 @@
     order = (column == 4 * ((row >> 2) & 31) + 2 * whose + (row & 1)).astype(BF16)
     plain = (iota((NVEC, NVEC), 0) == iota((NVEC, NVEC), 1)).astype(BF16)
     both = jnp.concatenate([plain, order], axis=0)
+    faces = []
     for rc in range(6):
         turned = lax.dot_general(both, v_ref[rc], NT, preferred_element_type=F32)
         for k in range(4):
             vt[rc, k] = turned[:128, k * 128 : k * 128 + 128]
         vo[rc] = turned[128:]
-        wide[rc] = v_ref[rc].astype(F32)
-        last = jnp.concatenate(list(layers(wide, rc, SIDE - 1)), axis=0).astype(BF16)
-        turned = lax.dot_general(order, last, NT, preferred_element_type=F32)
-        for d in range(3):
-            place = pl.ds((rc % 3) * FACE, FACE)
-            vl[d * 2 + rc // 3, :, place] = turned[:, d * FACE : d * FACE + FACE]
-    copy.wait()
+        faces.append([rows.astype(BF16) for rows in layers(wide, rc, SIDE - 1)])
+    for d in range(3):
+        for r in range(2):
+            last = jnp.concatenate([faces[r * 3 + c][d] for c in range(3)], axis=0)
+            vl[d * 2 + r] = lax.dot_general(order, last, NT, preferred_element_type=F32)
+    for copy in copies:
+        copy.wait()
+    for slot in range(3):
+        asked_ref[slot] = jnp.full((8, NVEC), dirs[slot], jnp.int32)
 
     def phase(site):
         lx, ly, lz = site >> 6, (site >> 3) & 7, site & 7
@@ -127,11 +134,14 @@
     for d, rows in enumerate(layers(ut, 0, SIDE - 1)):
         uf_ref[d] = rows
 
+
+def interior_kernel(vt, lt, ub, uf_ref, part0_ref, part1_ref, wide_ref, rt):
     upper = iota((16, 128), 1) >= 64
-    for d in range(3):
+
+    def products(d, h):
         for block in range(8):
             rows = pl.ds(block * 16, 16)
-            for k in range(4):
+            for k in (2 * h, 2 * h + 1):
                 lanes = pl.ds(k * 128, 128)
                 shifted = []
                 for rc in range(6):
@@ -149,12 +159,49 @@
                     lanes_out = pl.ds(i * SITES + k * 128, 128)
                     rt[d, rows, lanes_out] = dr.reshape(16, 128).astype(BF16)
                     rt[d, pl.ds(128 + block * 16, 16), lanes_out] = di.reshape(16, 128).astype(BF16)
-    for d in range(3):
-        full = lax.dot_general(lt[...], rt[d], NT, preferred_element_type=F32)
-        for half, out_ref in enumerate((part0_ref, part1_ref)):
-            re, im = complex_parts(full[half * 256 : half * 256 + 256])
-            out_ref[d * 2] = re
-            out_ref[d * 2 + 1] = im
+                yield
+
+    def contraction(sums, d, h):
+        for c in range(3):
+            lanes, stage = pl.ds((c * 2 + h) * 256, 256), (c + h) % 2
+            for m in range(2):
+                pltpu.matmul_push_rhs(rt[d, :, lanes], stage, m, transpose=True)
+            for n in range(4):
+                for m in range(2):
+                    rows = lt[pl.ds(m * 256 + n * 64, 64), lanes]
+                    pltpu.matmul_acc_lhs(sums[m][d][n], rows, stage if n == 0 else None)
+                yield
+
+    def finish(sums, d):
+        for m, out_ref in enumerate((part0_ref, part1_ref)):
+            for n in range(2):
+                rows = pl.ds(n * 64, 64)
+                top, bottom = pltpu.matmul_pop(sums[m][d][n]), pltpu.matmul_pop(sums[m][d][n + 2])
+                out_ref[d * 2, rows, :] = top[:, :128] + bottom[:, 128:]
+                out_ref[d * 2 + 1, rows, :] = top[:, 128:] - bottom[:, :128]
+
+    def widen(d, h):
+        for n in range(d * 18 + h * 9, d * 18 + h * 9 + 9):
+            wide_ref[n] = jnp.broadcast_to(uf_ref[d, :, n : n + 1], (FACE, NVEC))
+
+    def steps(sums):
+        work = iter(())
+        for d in range(3):
+            for h in range(2):
+                widen(d, h)
+                for n, _ in enumerate(products(d, h)):
+                    if n % 4 != 3:
+                        next(work, None)
+                for _ in work:
+                    pass
+                if h == 0 and d > 0:
+                    finish(sums, d - 1)
+                work = contraction(sums, d, h)
+        for _ in work:
+            pass
+        finish(sums, 2)
+
+    pl.run_scoped(steps, [[[pltpu.ACC(m)((64, 256), F32)] * 4 for _ in range(3)] for m in range(2)])
 
 
 def boundary_half(part_ref, lf_ref, right, chunk):
@@ -172,30 +219,25 @@
 
 def send_kernel(part_ref, lf_ref, uf_ref, x_ref, y_ref, z_ref, send_ref, right_ref, chunk):
     for d, layer_ref in enumerate((x_ref, y_ref, z_ref)):
-        layer = [layer_ref[rc].astype(F32) for rc in range(6)]
 
         def link(i, j):
             q = d * 18 + i * 6 + j * 2
-            return (
-                jnp.broadcast_to(uf_ref[d, :, q : q + 1], (FACE, NVEC)),
-                jnp.broadcast_to(uf_ref[d, :, q + 1 : q + 2], (FACE, NVEC)),
-            )
-
-        for i, dr, di in link_product(link, layer):
-            right_ref[d, pl.ds(i * FACE, FACE), pl.ds(0, NVEC)] = dr.astype(BF16)
-            right_ref[d, pl.ds(i * FACE, FACE), pl.ds(NVEC, NVEC)] = di.astype(BF16)
+            return uf_ref[q, rows, :], uf_ref[q + 1, rows, :]
+
+        for block in range(4):
+            rows = pl.ds(block * 16, 16)
+            layer = [layer_ref[rc, rows, :].astype(F32) for rc in range(6)]
+            for i, dr, di in link_product(link, layer):
+                out = pl.ds(i * FACE + block * 16, 16)
+                right_ref[d, out, pl.ds(0, NVEC)] = dr.astype(BF16)
+                right_ref[d, out, pl.ds(NVEC, NVEC)] = di.astype(BF16)
     boundary_half(part_ref, lf_ref, lambda d: right_ref[d], chunk)
     send_ref[...] = chunk[...].reshape(768, NVEC).astype(BF16)
 
 
-def keep_kernel(dir_hbm, part_ref, lf_ref, right_ref, keep_ref, asked_ref, dirs, sem, chunk):
-    copy = pltpu.make_async_copy(dir_hbm, dirs, sem)
-    copy.start()
+def keep_kernel(part_ref, lf_ref, right_ref, keep_ref, chunk):
     boundary_half(part_ref, lf_ref, lambda d: right_ref[d], chunk)
     keep_ref[...] = chunk[...].reshape(768, NVEC)
-    copy.wait()
-    for slot in range(3):
-        asked_ref[slot] = jnp.full((8, NVEC), dirs[slot], jnp.int32)
 
 
 def final_kernel(scale, asked_ref, got_ref, out_ref):
@@ -214,16 +256,15 @@
 
 
 def per_device(vectors, links, momenta, directions):
-    params = pltpu.CompilerParams(vmem_limit_bytes=48 * 1024 * 1024)
+    params = pltpu.CompilerParams(vmem_limit_bytes=16 * 1024 * 1024)
     field = vectors.reshape(6, SITES, NVEC)
     rows = links.transpose(0, 2, 3, 1, 4).reshape(27, 2, SITES)
     face = shape((6, FACE, NVEC), BF16)
-    held, *first = pl.pallas_call(
+    held, wide, *first = pl.pallas_call(
         layer_kernel,
-        out_shape=[shape((6, SITES, NVEC), BF16)] + [face] * 3,
+        out_shape=[shape((6, SITES, NVEC), BF16), shape((6, SITES, NVEC), F32)] + [face] * 3,
         in_specs=[VMEM],
-        out_specs=[VMEM] * 4,
-        scratch_shapes=[pltpu.VMEM((6, SITES, NVEC), F32)],
+        out_specs=[VMEM] * 5,
         input_output_aliases={0: 0},
         compiler_params=params,
     )(field)
@@ -233,29 +274,44 @@
     arrived = [lax.ppermute(a, "xyz", s) for a, s in zip(first, (step_x, step_y, step_z))]
     part = shape((6, NVEC, NVEC), F32)
     left = shape((3, 256, 3 * FACE), BF16)
-    part0, part1, left0, left1, link_face = pl.pallas_call(
-        interior_kernel,
-        out_shape=[part, part, left, left, shape((3, FACE, NVEC), F32)],
-        in_specs=[HBM] + [VMEM] * 2,
-        out_specs=[VMEM] * 5,
+    turned, left_all, spread, left0, left1, link_face, asked = pl.pallas_call(
+        factor_kernel,
+        out_shape=[
+            shape((6, 4, NVEC, 128), F32),
+            shape((512, 3 * SITES), BF16),
+            shape((54, 8, SITES), F32),
+            *[left, left],
+            shape((3, FACE, NVEC), F32),
+            shape((3, 8, NVEC), jnp.int32),
+        ],
+        in_specs=[HBM] * 2 + [VMEM] * 3,
+        out_specs=[VMEM] * 7,
         scratch_shapes=[
             pltpu.SMEM((2, 3), jnp.int32),
-            pltpu.SemaphoreType.DMA,
-            pltpu.VMEM((6, SITES, NVEC), F32),
-            pltpu.VMEM((6, 4, NVEC, 128), F32),
+            pltpu.SMEM((3,), jnp.int32),
+            pltpu.SemaphoreType.DMA((2,)),
             pltpu.VMEM((6, 256, SITES), F32),
             pltpu.VMEM((6, 256, 3 * FACE), F32),
-            pltpu.VMEM((512, 3 * SITES), BF16),
-            pltpu.VMEM((3, 256, 3 * SITES), BF16),
-            pltpu.VMEM((54, 8, SITES), F32),
             pltpu.VMEM((128, SITES), F32),
             pltpu.VMEM((1, SITES, 128), F32),
         ],
         compiler_params=params,
+    )(
+        pltpu.with_memory_space_constraint(momenta, pltpu.HBM),
+        pltpu.with_memory_space_constraint(directions, pltpu.HBM),
+        *[rows, held, wide],
+    )
+    part0, part1, link_wide = pl.pallas_call(
+        interior_kernel,
+        out_shape=[part, part, shape((54, FACE, NVEC), F32)],
+        in_specs=[VMEM] * 4,
+        out_specs=[VMEM] * 3,
+        scratch_shapes=[pltpu.VMEM((3, 256, 3 * SITES), BF16)],
+        compiler_params=params,
         cost_estimate=pl.CostEstimate(
             flops=2_000_000_000, bytes_accessed=4_000_000, transcendentals=0
         ),
-    )(pltpu.with_memory_space_constraint(momenta, pltpu.HBM), rows, held)
+    )(turned, left_all, spread, link_face)
     send, right = pl.pallas_call(
         send_kernel,
         out_shape=[shape((768, NVEC), BF16), shape((3, 3 * FACE, 256), BF16)],
@@ -263,20 +319,16 @@
         out_specs=[VMEM] * 2,
         scratch_shapes=[pltpu.VMEM((32, 24, NVEC), F32)],
         compiler_params=params,
-    )(part0, left0, link_face, *arrived)
+    )(part0, left0, link_wide, *arrived)
     other = lax.ppermute(send, "xyz", [(i, i ^ 1) for i in range(64)])
-    keep, asked = pl.pallas_call(
+    keep = pl.pallas_call(
         keep_kernel,
-        out_shape=[shape((768, NVEC), F32), shape((3, 8, NVEC), jnp.int32)],
-        in_specs=[HBM] + [VMEM] * 3,
-        out_specs=[VMEM] * 2,
-        scratch_shapes=[
-            pltpu.SMEM((3,), jnp.int32),
-            pltpu.SemaphoreType.DMA,
-            pltpu.VMEM((32, 24, NVEC), F32),
-        ],
-        compiler_params=params,
-    )(pltpu.with_memory_space_constraint(directions, pltpu.HBM), part1, left1, right)
+        out_shape=shape((768, NVEC), F32),
+        in_specs=[VMEM] * 3,
+        out_specs=VMEM,
+        scratch_shapes=[pltpu.VMEM((32, 24, NVEC), F32)],
+        compiler_params=params,
+    )(part1, left1, right)
     chip = (keep + other.astype(F32)).astype(BF16).reshape(32, 24, NVEC)
     groups = [[2 * c + core for c in range(32)] for core in range(2)]
     got = lax.all_to_all(chip, "xyz", 0, 0, axis_index_groups=groups, tiled=True)

time: 36.1 us -> 35.7 us (0.989)
  Pallas kernels: 8 us -> 7.42 us
  waiting for transfers between devices: 0.38 us -> 0.81 us
    ppermute x1, waiting for transfers between devices: 0.37 us -> 0.8 us  [per_device(): other = lax.ppermute(send, 'xyz', [(i, i ^ 1) for i in range(64)])]
    pallas_call x1, Pallas kernels: 0.9 us -> 0.49 us  [per_device(): pl.pallas_call(send_kernel, out_shape=[shape((768, NVEC), BF16), shape((3...]
    pallas_call x3 -> x4, Pallas kernels: 6.46 us -> 6.29 us  [the longest x1 3.23 us: per_device(): pl.pallas_call(interior_kernel, out_shape=[part, part, shape((54, FACE, N...]
  transfers between devices with their start and end apart: 4 -> 4, of which waited for: 1 -> 1; matrix products, arithmetic and copies ran while one was open for 0% -> 0% of each run, Pallas kernels for 18% -> 17%
where the time goes in v3:
time: 35.7 us; the launch traced here: 35.6 us
  blocking collectives  16.1 us (45%)
  starting transfers between devices  9.99 us (28%)
  Pallas kernels  7.42 us (21%)
  local copies, waits for them, and re-layouts  1.14 us (3%)
  waiting for transfers between devices  0.81 us (2%)
    all_to_all x1, blocking collectives, per_device(): lax.all_to_all(chip, 'xyz', 0, 0, axis_index_groups=groups, tiled=True)  16.1 us
    ppermute x3, starting transfers between devices, per_device(): lax.ppermute(a, 'xyz', s)  9.4 us
    pallas_call x1, Pallas kernels, per_device(): pl.pallas_call(interior_kernel, out_shape=[part, part, shape((54, FACE, N...  3.23 us
    pallas_call x1, Pallas kernels, per_device(): pl.pallas_call(factor_kernel, out_shape=[shape((6, 4, NVEC, 128), F32), s...  2.64 us
    unnamed x3, local copies, waits for them, and re-layouts  1.14 us
    ppermute x1, waiting for transfers between devices, per_device(): other = lax.ppermute(send, 'xyz', [(i, i ^ 1) for i in range(64)])  0.8 us
  transfers between devices with their start and end apart: 4, of which 1 were waited for; matrix products, arithmetic and copies ran while one was open for 0% of the time, Pallas kernels for 17%

profile of v3, /device:TPU:8, one launch (start us, length us, event | category | flops | bytes accessed | tf_op | source)
XLA Modules:
  0.0 35.6 jit_solution(4991895539230840923)
XLA Ops:
  0.0 0.0 copy-start
  0.0 1.1 %copy.8 = bf16[2,3,512,128]{3,2,1,0:T(8,128)(2,1)S(1)} copy(bf16[2,3,512,128]{3,2,1,0:T(8,128)(2,1)} %param.4) | data formatting | bytes 1572864
  1.1 0.2 shard_map.46
  1.3 6.4 %collective-permute-start = (bf16[6,64,128]{2,1,0:T(8,128)(2,1)S(1)}, bf16[6,64,128]{2,1,0:T(8,128)(2,1)S(1)}, u32[]{:S(2)}, u32[]{:S(2)}) collective-permute-start(bf16[6,64,128]{2,1,0:T(8,128)(2,1)S(1)} %get-tuple-element.34), channel_id=1, source_target_pairs={{0,48},{1,49},{2,50},{3,51},{4,52},{5,53},{6,54},{7,55},{8,56},{9,... | collective-permute-start | bytes 294920 | tf_op jit(solution)/shard_map/ppermute | solution.py:274
  7.7 3.0 %collective-permute-start.1 = (bf16[6,64,128]{2,1,0:T(8,128)(2,1)S(1)}, bf16[6,64,128]{2,1,0:T(8,128)(2,1)S(1)}, u32[]{:S(2)}, u32[]{:S(2)}) collective-permute-start(bf16[6,64,128]{2,1,0:T(8,128)(2,1)S(1)} %get-tuple-element.35), channel_id=1, source_target_pairs={{0,4},{1,5},{2,6},{3,7},{4,8},{5,9},{6,10},{7,11},{8,12},{9,13},{1... | collective-permute-start | bytes 294920 | tf_op jit(solution)/shard_map/ppermute | solution.py:274
  10.7 0.0 collective-permute-start.2
  10.7 0.0 copy-done
  10.7 2.6 %shard_map.47 = (f32[6,4,128,128]{3,2,1,0:T(8,128)S(1)}, bf16[512,1536]{1,0:T(8,128)(2,1)S(1)}, f32[54,8,512]{2,1,0:T(8,128)S(1)}, bf16[3,256,192]{2,1,0:T(8,128...) custom-call(s32[2,3]{1,0:T(2,128)} %mom_hbm.1, s32[3]{0:T(128)} %dir_hbm.1, ...), custom_call_target="tpu_custom_call" | custom-call | tf_op jit(solution)/shard_map/pallas_call | solution.py:277
  13.4 3.2 %shard_map.48 = (f32[6,128,128]{2,1,0:T(8,128)S(1)}, f32[6,128,128]{2,1,0:T(8,128)S(1)}, f32[54,64,128]{2,1,0:T(8,128)S(1)}) custom-call(f32[6,4,128,128]{3,2,1,0:T(8,128)S(1)} %get-tuple-element.25.vt, bf16[512,1536]{1,0:T(8,128)(2,1)S(1)} %get-tuple-element.26.lt, f32[54,8,512]{2,1,0:T(8,128)S(1)} %get-tuple-element.27.ub, ...), custom_call_target="tpu_custom_call" | custom-call | flops 2000000000 | bytes 4000000 | tf_op jit(solution)/shard_map/pallas_call | solution.py:304
  16.6 0.0 collective-permute-done.x_ref
  16.6 0.0 collective-permute-done.1.y_ref
  16.6 0.0 collective-permute-done.2.z_ref
  16.6 0.5 %shard_map.49 = (bf16[768,128]{1,0:T(8,128)(2,1)S(1)}, bf16[3,192,256]{2,1,0:T(8,128)(2,1)S(1)}) custom-call(f32[6,128,128]{2,1,0:T(8,128)S(1)} %get-tuple-element.31.part_ref, bf16[3,256,192]{2,1,0:T(8,128)(2,1)S(1)} %get-tuple-element.32.lf_ref, f32[54,64,128]{2,1,0:T(8,128)S(1)} %get-tuple-element.33.uf_ref, ...), custom_call_target="tpu_custom_call" | custom-call | tf_op jit(solution)/shard_map/pallas_call | solution.py:315
  17.1 0.6 %collective-permute-start.3 = (bf16[768,128]{1,0:T(8,128)(2,1)S(1)}, bf16[768,128]{1,0:T(8,128)(2,1)S(1)}, u32[]{:S(2)}, u32[]{:S(2)}) collective-permute-start(bf16[768,128]{1,0:T(8,128)(2,1)S(1)} %get-tuple-element.38), channel_id=1, source_target_pairs={{0,1},{1,0},{2,3},{3,2},{4,5},{5,4},{6,7},{7,6},{8,9},{9,8},{10,11... | collective-permute-start | bytes 589832 | tf_op jit(solution)/shard_map/ppermute | solution.py:323
  17.7 0.3 shard_map.50
  18.0 0.8 %collective-permute-done.3 = bf16[768,128]{1,0:T(8,128)(2,1)S(1)} collective-permute-done((bf16[768,128]{1,0:T(8,128)(2,1)S(1)}, bf16[768,128]{1,0:T(8,128)(2,1)S(1)}, u32[]{:S(2)}, u32[]{:S(2)}) %collective-permute-start.3) | collective-permute-done | bytes 196640 | tf_op jit(solution)/shard_map/ppermute | solution.py:323
  18.8 16.1 %all_to_all.5.got_ref = bf16[32,24,128]{2,1,0:T(8,128)(2,1)S(1)} all-to-all(bf16[32,24,128]{2,1,0:T(8,128)(2,1)S(1)} %bitcast.7), channel_id=1, replica_groups={{0,2,4,6,8,10,12,14,16,18,20,22,24,26,28,30,32,34,36,38,40,42,44,46,48,..., dimensions={0} | all-to-all | bytes 393216 | tf_op jit(solution)/shard_map/all_to_all | solution.py:334
  34.9 0.6 %shard_map.51 = f32[2,3,2,2,128]{4,3,2,1,0:T(2,128)} custom-call(s32[3,8,128]{2,1,0:T(8,128)S(1)} %get-tuple-element.24.asked_ref, bf16[32,24,128]{2,1,0:T(8,128)(2,1)S(1)} %all_to_all.5.got_ref), custom_call_target="tpu_custom_call" | custom-call | tf_op jit(solution)/shard_map/pallas_call | solution.py:335
  (1 shorter events, 0.0 us)
Async XLA Ops:
  0.0 10.7 %copy-start = (bf16[3,2,3,3,512]{4,1,3,2,0:T(2,128)(2,1)S(1)}, bf16[3,2,3,3,512]{4,1,3,2,0:T(2,128)(2,1)}, u32[]{:S(2)}) copy-start(bf16[3,2,3,3,512]{4,1,3,2,0:T(2,128)(2,1)} %param.5) | copy-start | bytes 165892
  1.3 15.3 %collective-permute-start = (bf16[6,64,128]{2,1,0:T(8,128)(2,1)S(1)}, bf16[6,64,128]{2,1,0:T(8,128)(2,1)S(1)}, u32[]{:S(2)}, u32[]{:S(2)}) collective-permute-start(bf16[6,64,128]{2,1,0:T(8,128)(2,1)S(1)} %get-tuple-element.34), channel_id=1, source_target_pairs={{0,48},{1,49},{2,50},{3,51},{4,52},{5,53},{6,54},{7,55},{8,56},{9,... | collective-permute-start | bytes 294920 | tf_op jit(solution)/shard_map/ppermute | solution.py:274
  7.7 8.9 %collective-permute-start.1 = (bf16[6,64,128]{2,1,0:T(8,128)(2,1)S(1)}, bf16[6,64,128]{2,1,0:T(8,128)(2,1)S(1)}, u32[]{:S(2)}, u32[]{:S(2)}) collective-permute-start(bf16[6,64,128]{2,1,0:T(8,128)(2,1)S(1)} %get-tuple-element.35), channel_id=1, source_target_pairs={{0,4},{1,5},{2,6},{3,7},{4,8},{5,9},{6,10},{7,11},{8,12},{9,13},{1... | collective-permute-start | bytes 294920 | tf_op jit(solution)/shard_map/ppermute | solution.py:274
  10.7 5.9 %collective-permute-start.2 = (bf16[6,64,128]{2,1,0:T(8,128)(2,1)S(1)}, bf16[6,64,128]{2,1,0:T(8,128)(2,1)S(1)}, u32[]{:S(2)}, u32[]{:S(2)}) collective-permute-start(bf16[6,64,128]{2,1,0:T(8,128)(2,1)S(1)} %get-tuple-element.36), channel_id=1, source_target_pairs={{0,3},{1,0},{2,1},{3,2},{4,7},{5,4},{6,5},{7,6},{8,11},{9,8},{10,9... | collective-permute-start | bytes 294920 | tf_op jit(solution)/shard_map/ppermute | solution.py:274
  17.1 1.7 %collective-permute-start.3 = (bf16[768,128]{1,0:T(8,128)(2,1)S(1)}, bf16[768,128]{1,0:T(8,128)(2,1)S(1)}, u32[]{:S(2)}, u32[]{:S(2)}) collective-permute-start(bf16[768,128]{1,0:T(8,128)(2,1)S(1)} %get-tuple-element.38), channel_id=1, source_target_pairs={{0,1},{1,0},{2,3},{3,2},{4,5},{5,4},{6,7},{7,6},{8,9},{9,8},{10,11... | collective-permute-start | bytes 589832 | tf_op jit(solution)/shard_map/ppermute | solution.py:323

commit v4 on v3

--- a/solution.py
+++ b/solution.py
@@ -28,6 +28,9 @@
     return ((SIDE - 1) * 64 + face, hi * 64 + (SIDE - 1) * 8 + lo, face * 8 + SIDE - 1)[direction]
 
 
+PLACES = (0, 4, 1, 5, 2, 6, 3, 7)
+
+
 def layers(ref, index, layer):
     yield ref[index, pl.ds(layer * 64, 64), :]
     yield jnp.concatenate([ref[index, pl.ds(n * 64 + layer * 8, 8), :] for n in range(8)], axis=0)
@@ -50,6 +53,17 @@
             tr, ti = ur * vr - ui * vi, ui * vr + ur * vi
             dr, di = (tr, ti) if dr is None else (dr + tr, di + ti)
         yield i, dr, di
+
+
+def link_product_of_three(link, shifted):
+    both = [shifted[j] + shifted[3 + j] for j in range(3)]
+    for i in range(3):
+        sums = None
+        for j in range(3):
+            real, less, more = link(i, j)
+            terms = (real * both[j], less * shifted[j], more * shifted[3 + j])
+            sums = terms if sums is None else [a + b for a, b in zip(sums, terms)]
+        yield i, sums[0] - sums[2], sums[0] + sums[1]
 
 
 def complex_parts(full):
@@ -77,7 +91,8 @@
     both = jnp.concatenate([plain, order], axis=0)
     faces = []
     for rc in range(6):
-        turned = lax.dot_general(both, v_ref[rc], NT, preferred_element_type=F32)
+        field = jnp.concatenate([v_ref[rc, pl.ds(n * 64, 64), :] for n in PLACES], axis=0)
+        turned = lax.dot_general(both, field, NT, preferred_element_type=F32)
         for k in range(4):
             vt[rc, k] = turned[:128, k * 128 : k * 128 + 128]
         vo[rc] = turned[128:]
@@ -105,7 +120,8 @@
         left = (cosine * re - sine * im).reshape(-1, width).astype(BF16)
         return left, (sine * re + cosine * im).reshape(-1, width).astype(BF16)
 
-    site = iota((8, SITES), 1)
+    lane = iota((8, SITES), 1)
+    site = (((lane >> 7) + 4 * ((lane >> 6) & 1)) << 6) + (lane & 63)
     turn = phase(site)
     for block in range(16):
         rows = pl.ds(block * 16, 16)
@@ -123,12 +139,15 @@
 
     inner = [(n < SIDE - 1).astype(F32) for n in (site >> 6, (site >> 3) & 7, site & 7)]
     us[pl.ds(54, 74), :] = jnp.zeros((74, SITES), F32)
+    for n in range(27):
+        us[pl.ds(n * 2, 2), :] = u[n].astype(F32)
+    placed = jnp.concatenate([us[pl.ds(0, 56), n * 64 : n * 64 + 64] for n in PLACES], axis=1)
     for d in range(3):
         for ij in range(9):
-            pair = u[d * 9 + ij].astype(F32)
-            us[pl.ds((d * 9 + ij) * 2, 2), :] = pair
-            for r in range(2):
-                ub[d * 18 + ij * 2 + r] = pair[r : r + 1] * inner[d]
+            n = (d * 9 + ij) * 2
+            real, imag = placed[n : n + 1] * inner[d], placed[n + 1 : n + 2] * inner[d]
+            for n, row in enumerate((real, imag - real, imag + real)):
+                ub[d * 27 + ij * 3 + n] = row
     for k in range(4):
         ut[0, pl.ds(k * 128, 128), :] = us[:, k * 128 : k * 128 + 128].T
     for d, rows in enumerate(layers(ut, 0, SIDE - 1)):
@@ -136,8 +155,6 @@
 
 
 def interior_kernel(vt, lt, ub, uf_ref, part0_ref, part1_ref, wide_ref, rt):
-    upper = iota((16, 128), 1) >= 64
-
     def products(d, h):
         for block in range(8):
             rows = pl.ds(block * 16, 16)
@@ -145,17 +162,19 @@
                 lanes = pl.ds(k * 128, 128)
                 shifted = []
                 for rc in range(6):
-                    here = pltpu.roll(vt[rc, k, rows, :], (64, 120, 127)[d], 1)
                     if d == 0 and k < 3:
-                        after = pltpu.roll(vt[rc, k + 1, rows, :], 64, 1)
-                        here = jnp.where(upper, after, here)
+                        here = vt[rc, k + 1, rows, :]
+                    elif d == 0:
+                        here = pltpu.roll(vt[rc, 0, rows, :], 64, 1)
+                    else:
+                        here = pltpu.roll(vt[rc, k, rows, :], (0, 120, 127)[d], 1)
                     shifted.append(here.reshape(2, 8, 128))
 
                 def link(i, j):
-                    q = d * 18 + i * 6 + j * 2
-                    return ub[q, :, lanes][None], ub[q + 1, :, lanes][None]
-
-                for i, dr, di in link_product(link, shifted):
+                    q = d * 27 + i * 9 + j * 3
+                    return [ub[q + n, :, lanes][None] for n in range(3)]
+
+                for i, dr, di in link_product_of_three(link, shifted):
                     lanes_out = pl.ds(i * SITES + k * 128, 128)
                     rt[d, rows, lanes_out] = dr.reshape(16, 128).astype(BF16)
                     rt[d, pl.ds(128 + block * 16, 16), lanes_out] = di.reshape(16, 128).astype(BF16)
@@ -163,22 +182,21 @@
 
     def contraction(sums, d, h):
         for c in range(3):
-            lanes, stage = pl.ds((c * 2 + h) * 256, 256), (c + h) % 2
-            for m in range(2):
-                pltpu.matmul_push_rhs(rt[d, :, lanes], stage, m, transpose=True)
-            for n in range(4):
-                for m in range(2):
-                    rows = lt[pl.ds(m * 256 + n * 64, 64), lanes]
-                    pltpu.matmul_acc_lhs(sums[m][d][n], rows, stage if n == 0 else None)
+            lanes, m, stage = pl.ds((c * 2 + h) * 256, 256), (c + h) % 2, c // 2
+            pltpu.matmul_push_rhs(rt[d, :, lanes], stage, m, transpose=True)
+            for n in range(8):
+                rows = lt[pl.ds(n * 64, 64), lanes]
+                pltpu.matmul_acc_lhs(sums[m][n], rows, stage if n == 0 else None)
                 yield
 
     def finish(sums, d):
-        for m, out_ref in enumerate((part0_ref, part1_ref)):
+        rows = [pltpu.matmul_pop(sums[0][n]) + pltpu.matmul_pop(sums[1][n]) for n in range(8)]
+        for half, out_ref in enumerate((part0_ref, part1_ref)):
             for n in range(2):
-                rows = pl.ds(n * 64, 64)
-                top, bottom = pltpu.matmul_pop(sums[m][d][n]), pltpu.matmul_pop(sums[m][d][n + 2])
-                out_ref[d * 2, rows, :] = top[:, :128] + bottom[:, 128:]
-                out_ref[d * 2 + 1, rows, :] = top[:, 128:] - bottom[:, :128]
+                place = pl.ds(n * 64, 64)
+                top, bottom = rows[half * 4 + n], rows[half * 4 + n + 2]
+                out_ref[d * 2, place, :] = top[:, :128] + bottom[:, 128:]
+                out_ref[d * 2 + 1, place, :] = top[:, 128:] - bottom[:, :128]
 
     def widen(d, h):
         for n in range(d * 18 + h * 9, d * 18 + h * 9 + 9):
@@ -190,7 +208,8 @@
             for h in range(2):
                 widen(d, h)
                 for n, _ in enumerate(products(d, h)):
-                    if n % 4 != 3:
+                    next(work, None)
+                    if n % 2:
                         next(work, None)
                 for _ in work:
                     pass
@@ -201,7 +220,7 @@
             pass
         finish(sums, 2)
 
-    pl.run_scoped(steps, [[[pltpu.ACC(m)((64, 256), F32)] * 4 for _ in range(3)] for m in range(2)])
+    pl.run_scoped(steps, [[pltpu.ACC(m)((64, 256), F32)] * 8 for m in range(2)])
 
 
 def boundary_half(part_ref, lf_ref, right, chunk):
@@ -279,7 +298,7 @@
         out_shape=[
             shape((6, 4, NVEC, 128), F32),
             shape((512, 3 * SITES), BF16),
-            shape((54, 8, SITES), F32),
+            shape((81, 8, SITES), F32),
             *[left, left],
             shape((3, FACE, NVEC), F32),
             shape((3, 8, NVEC), jnp.int32),

time: 35.7 us -> 35.7 us (level)
  Pallas kernels: 7.42 us -> 7 us
  blocking collectives: 16.1 us -> 16.5 us
    pallas_call x1, Pallas kernels: 3.23 us -> 2.85 us  [per_device(): pl.pallas_call(interior_kernel, out_shape=[part, part, shape((54, FACE, N...]
    all_to_all x1, blocking collectives: 16.1 us -> 16.5 us  [per_device(): lax.all_to_all(chip, 'xyz', 0, 0, axis_index_groups=groups, tiled=True)]
  transfers between devices with their start and end apart: 4 -> 4, of which waited for: 1 -> 1; matrix products, arithmetic and copies ran while one was open for 0% -> 0% of each run, Pallas kernels for 17% -> 16%
where the time goes in v4:
time: 35.7 us; the launch traced here: 35.5 us
  blocking collectives  16.5 us (46%)
  starting transfers between devices  10 us (28%)
  Pallas kernels  7 us (20%)
  local copies, waits for them, and re-layouts  1.14 us (3%)
  waiting for transfers between devices  0.81 us (2%)
    all_to_all x1, blocking collectives, per_device(): lax.all_to_all(chip, 'xyz', 0, 0, axis_index_groups=groups, tiled=True)  16.5 us
    ppermute x3, starting transfers between devices, per_device(): lax.ppermute(a, 'xyz', s)  9.4 us
    pallas_call x1, Pallas kernels, per_device(): pl.pallas_call(interior_kernel, out_shape=[part, part, shape((54, FACE, N...  2.85 us
    pallas_call x1, Pallas kernels, per_device(): pl.pallas_call(factor_kernel, out_shape=[shape((6, 4, NVEC, 128), F32), s...  2.6 us
    unnamed x3, local copies, waits for them, and re-layouts  1.14 us
    ppermute x1, waiting for transfers between devices, per_device(): other = lax.ppermute(send, 'xyz', [(i, i ^ 1) for i in range(64)])  0.81 us
  transfers between devices with their start and end apart: 4, of which 1 were waited for; matrix products, arithmetic and copies ran while one was open for 0% of the time, Pallas kernels for 16%

profile of v4, /device:TPU:8, one launch (start us, length us, event | category | flops | bytes accessed | tf_op | source)
XLA Modules:
  0.0 35.5 jit_solution(5119160877752616369)
XLA Ops:
  0.0 0.0 copy-start
  0.0 1.1 %copy.8 = bf16[2,3,512,128]{3,2,1,0:T(8,128)(2,1)S(1)} copy(bf16[2,3,512,128]{3,2,1,0:T(8,128)(2,1)} %param.4) | data formatting | bytes 1572864
  1.1 0.2 shard_map.46
  1.3 6.4 %collective-permute-start = (bf16[6,64,128]{2,1,0:T(8,128)(2,1)S(1)}, bf16[6,64,128]{2,1,0:T(8,128)(2,1)S(1)}, u32[]{:S(2)}, u32[]{:S(2)}) collective-permute-start(bf16[6,64,128]{2,1,0:T(8,128)(2,1)S(1)} %get-tuple-element.34), channel_id=1, source_target_pairs={{0,48},{1,49},{2,50},{3,51},{4,52},{5,53},{6,54},{7,55},{8,56},{9,... | collective-permute-start | bytes 294920 | tf_op jit(solution)/shard_map/ppermute | solution.py:293
  7.7 3.0 %collective-permute-start.1 = (bf16[6,64,128]{2,1,0:T(8,128)(2,1)S(1)}, bf16[6,64,128]{2,1,0:T(8,128)(2,1)S(1)}, u32[]{:S(2)}, u32[]{:S(2)}) collective-permute-start(bf16[6,64,128]{2,1,0:T(8,128)(2,1)S(1)} %get-tuple-element.35), channel_id=1, source_target_pairs={{0,4},{1,5},{2,6},{3,7},{4,8},{5,9},{6,10},{7,11},{8,12},{9,13},{1... | collective-permute-start | bytes 294920 | tf_op jit(solution)/shard_map/ppermute | solution.py:293
  10.7 0.0 collective-permute-start.2
  10.7 0.0 copy-done
  10.7 2.6 %shard_map.47 = (f32[6,4,128,128]{3,2,1,0:T(8,128)S(1)}, bf16[512,1536]{1,0:T(8,128)(2,1)S(1)}, f32[81,8,512]{2,1,0:T(8,128)S(1)}, bf16[3,256,192]{2,1,0:T(8,128...) custom-call(s32[2,3]{1,0:T(2,128)} %mom_hbm.1, s32[3]{0:T(128)} %dir_hbm.1, ...), custom_call_target="tpu_custom_call" | custom-call | tf_op jit(solution)/shard_map/pallas_call | solution.py:296
  13.3 2.9 %shard_map.48 = (f32[6,128,128]{2,1,0:T(8,128)S(1)}, f32[6,128,128]{2,1,0:T(8,128)S(1)}, f32[54,64,128]{2,1,0:T(8,128)S(1)}) custom-call(f32[6,4,128,128]{3,2,1,0:T(8,128)S(1)} %get-tuple-element.25.vt, bf16[512,1536]{1,0:T(8,128)(2,1)S(1)} %get-tuple-element.26.lt, f32[81,8,512]{2,1,0:T(8,128)S(1)} %get-tuple-element.27.ub, ...), custom_call_target="tpu_custom_call" | custom-call | flops 2000000000 | bytes 4000000 | tf_op jit(solution)/shard_map/pallas_call | solution.py:323
  16.2 0.0 collective-permute-done.x_ref
  16.2 0.0 collective-permute-done.1.y_ref
  16.2 0.0 collective-permute-done.2.z_ref
  16.2 0.5 %shard_map.49 = (bf16[768,128]{1,0:T(8,128)(2,1)S(1)}, bf16[3,192,256]{2,1,0:T(8,128)(2,1)S(1)}) custom-call(f32[6,128,128]{2,1,0:T(8,128)S(1)} %get-tuple-element.31.part_ref, bf16[3,256,192]{2,1,0:T(8,128)(2,1)S(1)} %get-tuple-element.32.lf_ref, f32[54,64,128]{2,1,0:T(8,128)S(1)} %get-tuple-element.33.uf_ref, ...), custom_call_target="tpu_custom_call" | custom-call | tf_op jit(solution)/shard_map/pallas_call | solution.py:334
  16.7 0.6 %collective-permute-start.3 = (bf16[768,128]{1,0:T(8,128)(2,1)S(1)}, bf16[768,128]{1,0:T(8,128)(2,1)S(1)}, u32[]{:S(2)}, u32[]{:S(2)}) collective-permute-start(bf16[768,128]{1,0:T(8,128)(2,1)S(1)} %get-tuple-element.38), channel_id=1, source_target_pairs={{0,1},{1,0},{2,3},{3,2},{4,5},{5,4},{6,7},{7,6},{8,9},{9,8},{10,11... | collective-permute-start | bytes 589832 | tf_op jit(solution)/shard_map/ppermute | solution.py:342
  17.3 0.3 shard_map.50
  17.6 0.8 %collective-permute-done.3 = bf16[768,128]{1,0:T(8,128)(2,1)S(1)} collective-permute-done((bf16[768,128]{1,0:T(8,128)(2,1)S(1)}, bf16[768,128]{1,0:T(8,128)(2,1)S(1)}, u32[]{:S(2)}, u32[]{:S(2)}) %collective-permute-start.3) | collective-permute-done | bytes 196640 | tf_op jit(solution)/shard_map/ppermute | solution.py:342
  18.4 16.5 %all_to_all.5.got_ref = bf16[32,24,128]{2,1,0:T(8,128)(2,1)S(1)} all-to-all(bf16[32,24,128]{2,1,0:T(8,128)(2,1)S(1)} %bitcast.7), channel_id=1, replica_groups={{0,2,4,6,8,10,12,14,16,18,20,22,24,26,28,30,32,34,36,38,40,42,44,46,48,..., dimensions={0} | all-to-all | bytes 393216 | tf_op jit(solution)/shard_map/all_to_all | solution.py:353
  34.9 0.6 %shard_map.51 = f32[2,3,2,2,128]{4,3,2,1,0:T(2,128)} custom-call(s32[3,8,128]{2,1,0:T(8,128)S(1)} %get-tuple-element.24.asked_ref, bf16[32,24,128]{2,1,0:T(8,128)(2,1)S(1)} %all_to_all.5.got_ref), custom_call_target="tpu_custom_call" | custom-call | tf_op jit(solution)/shard_map/pallas_call | solution.py:354
  (1 shorter events, 0.0 us)
Async XLA Ops:
  0.0 10.7 %copy-start = (bf16[3,2,3,3,512]{4,1,3,2,0:T(2,128)(2,1)S(1)}, bf16[3,2,3,3,512]{4,1,3,2,0:T(2,128)(2,1)}, u32[]{:S(2)}) copy-start(bf16[3,2,3,3,512]{4,1,3,2,0:T(2,128)(2,1)} %param.5) | copy-start | bytes 165892
  1.3 14.9 %collective-permute-start = (bf16[6,64,128]{2,1,0:T(8,128)(2,1)S(1)}, bf16[6,64,128]{2,1,0:T(8,128)(2,1)S(1)}, u32[]{:S(2)}, u32[]{:S(2)}) collective-permute-start(bf16[6,64,128]{2,1,0:T(8,128)(2,1)S(1)} %get-tuple-element.34), channel_id=1, source_target_pairs={{0,48},{1,49},{2,50},{3,51},{4,52},{5,53},{6,54},{7,55},{8,56},{9,... | collective-permute-start | bytes 294920 | tf_op jit(solution)/shard_map/ppermute | solution.py:293
  7.7 8.5 %collective-permute-start.1 = (bf16[6,64,128]{2,1,0:T(8,128)(2,1)S(1)}, bf16[6,64,128]{2,1,0:T(8,128)(2,1)S(1)}, u32[]{:S(2)}, u32[]{:S(2)}) collective-permute-start(bf16[6,64,128]{2,1,0:T(8,128)(2,1)S(1)} %get-tuple-element.35), channel_id=1, source_target_pairs={{0,4},{1,5},{2,6},{3,7},{4,8},{5,9},{6,10},{7,11},{8,12},{9,13},{1... | collective-permute-start | bytes 294920 | tf_op jit(solution)/shard_map/ppermute | solution.py:293
  10.7 5.5 %collective-permute-start.2 = (bf16[6,64,128]{2,1,0:T(8,128)(2,1)S(1)}, bf16[6,64,128]{2,1,0:T(8,128)(2,1)S(1)}, u32[]{:S(2)}, u32[]{:S(2)}) collective-permute-start(bf16[6,64,128]{2,1,0:T(8,128)(2,1)S(1)} %get-tuple-element.36), channel_id=1, source_target_pairs={{0,3},{1,0},{2,1},{3,2},{4,7},{5,4},{6,5},{7,6},{8,11},{9,8},{10,9... | collective-permute-start | bytes 294920 | tf_op jit(solution)/shard_map/ppermute | solution.py:293
  16.7 1.7 %collective-permute-start.3 = (bf16[768,128]{1,0:T(8,128)(2,1)S(1)}, bf16[768,128]{1,0:T(8,128)(2,1)S(1)}, u32[]{:S(2)}, u32[]{:S(2)}) collective-permute-start(bf16[768,128]{1,0:T(8,128)(2,1)S(1)} %get-tuple-element.38), channel_id=1, source_target_pairs={{0,1},{1,0},{2,3},{3,2},{4,5},{5,4},{6,7},{7,6},{8,9},{9,8},{10,11... | collective-permute-start | bytes 589832 | tf_op jit(solution)/shard_map/ppermute | solution.py:342

commit v5 on v4

--- a/solution.py
+++ b/solution.py
@@ -223,47 +223,55 @@
     pl.run_scoped(steps, [[pltpu.ACC(m)((64, 256), F32)] * 8 for m in range(2)])
 
 
-def boundary_half(part_ref, lf_ref, right, chunk):
+def boundary_half(d, part_ref, lf_ref, right):
     low = iota((16, 8, NVEC), 1) < 4
-    for d in range(3):
-        term = jnp.dot(lf_ref[d], right(d), preferred_element_type=F32)
-        re, im = complex_parts(term)
-        re = (part_ref[d * 2] + re).reshape(16, 8, NVEC)
-        im = (part_ref[d * 2 + 1] + im).reshape(16, 8, NVEC)
-        even = jnp.where(low, re, pltpu.roll(im, 4, 1))
-        odd = jnp.where(low, pltpu.roll(re, 4, 1), im)
-        pairs = jnp.stack([even, odd], axis=1).reshape(32, 8, NVEC)
-        chunk[:, pl.ds(d * 8, 8), :] = pairs
-
-
-def send_kernel(part_ref, lf_ref, uf_ref, x_ref, y_ref, z_ref, send_ref, right_ref, chunk):
-    for d, layer_ref in enumerate((x_ref, y_ref, z_ref)):
-
-        def link(i, j):
-            q = d * 18 + i * 6 + j * 2
-            return uf_ref[q, rows, :], uf_ref[q + 1, rows, :]
-
-        for block in range(4):
-            rows = pl.ds(block * 16, 16)
-            layer = [layer_ref[rc, rows, :].astype(F32) for rc in range(6)]
-            for i, dr, di in link_product(link, layer):
-                out = pl.ds(i * FACE + block * 16, 16)
-                right_ref[d, out, pl.ds(0, NVEC)] = dr.astype(BF16)
-                right_ref[d, out, pl.ds(NVEC, NVEC)] = di.astype(BF16)
-    boundary_half(part_ref, lf_ref, lambda d: right_ref[d], chunk)
+    re, im = complex_parts(jnp.dot(lf_ref[d], right, preferred_element_type=F32))
+    re = (part_ref[d * 2] + re).reshape(16, 8, NVEC)
+    im = (part_ref[d * 2 + 1] + im).reshape(16, 8, NVEC)
+    even = jnp.where(low, re, pltpu.roll(im, 4, 1))
+    odd = jnp.where(low, pltpu.roll(re, 4, 1), im)
+    return jnp.stack([even, odd], axis=1).reshape(32, 8, NVEC)
+
+
+def face_products(d, uf_ref, layer_ref, right_ref, place):
+    def link(i, j):
+        q = d * 18 + i * 6 + j * 2
+        return uf_ref[q, rows, :], uf_ref[q + 1, rows, :]
+
+    for block in range(4):
+        rows = pl.ds(block * 16, 16)
+        layer = [layer_ref[rc, rows, :].astype(F32) for rc in range(6)]
+        for i, dr, di in link_product(link, layer):
+            out = pl.ds(i * FACE + block * 16, 16)
+            right_ref[place, out, pl.ds(0, NVEC)] = dr.astype(BF16)
+            right_ref[place, out, pl.ds(NVEC, NVEC)] = di.astype(BF16)
+
+
+def early_kernel(part_ref, lf_ref, uf_ref, x_ref, z_ref, early_ref, right_ref):
+    for n, (d, layer_ref) in enumerate(((0, x_ref), (2, z_ref))):
+        face_products(d, uf_ref, layer_ref, right_ref, n)
+        early_ref[:, pl.ds(n * 8, 8), :] = boundary_half(d, part_ref, lf_ref, right_ref[n])
+
+
+def send_kernel(part_ref, lf_ref, uf_ref, y_ref, early_ref, send_ref, right_ref, chunk):
+    face_products(1, uf_ref, y_ref, right_ref, 0)
+    chunk[:, pl.ds(0, 16), :] = early_ref[...]
+    chunk[:, pl.ds(16, 8), :] = boundary_half(1, part_ref, lf_ref, right_ref[0])
     send_ref[...] = chunk[...].reshape(768, NVEC).astype(BF16)
 
 
-def keep_kernel(part_ref, lf_ref, right_ref, keep_ref, chunk):
-    boundary_half(part_ref, lf_ref, lambda d: right_ref[d], chunk)
+def keep_kernel(part_ref, lf_ref, right_ref, right_y_ref, keep_ref, chunk):
+    for n, d in enumerate((0, 2, 1)):
+        right = right_y_ref[0] if d == 1 else right_ref[n]
+        chunk[:, pl.ds(n * 8, 8), :] = boundary_half(d, part_ref, lf_ref, right)
     keep_ref[...] = chunk[...].reshape(768, NVEC)
 
 
 def final_kernel(scale, asked_ref, got_ref, out_ref):
     rows = jnp.sum(got_ref[...].astype(F32), axis=0) * scale
     for slot in range(3):
-        chosen = jnp.where(asked_ref[slot] == 1, rows[8:16], rows[0:8])
-        chosen = jnp.where(asked_ref[slot] == 2, rows[16:24], chosen)
+        chosen = jnp.where(asked_ref[slot] == 2, rows[8:16], rows[0:8])
+        chosen = jnp.where(asked_ref[slot] == 1, rows[16:24], chosen)
         for o in range(2):
             for p in range(2):
                 t = o * 4 + p * 2
@@ -331,23 +339,30 @@
             flops=2_000_000_000, bytes_accessed=4_000_000, transcendentals=0
         ),
     )(turned, left_all, spread, link_face)
-    send, right = pl.pallas_call(
+    early, right = pl.pallas_call(
+        early_kernel,
+        out_shape=[shape((32, 16, NVEC), F32), shape((2, 3 * FACE, 256), BF16)],
+        in_specs=[VMEM] * 5,
+        out_specs=[VMEM] * 2,
+        compiler_params=params,
+    )(part0, left0, link_wide, arrived[0], arrived[2])
+    send, right_y = pl.pallas_call(
         send_kernel,
-        out_shape=[shape((768, NVEC), BF16), shape((3, 3 * FACE, 256), BF16)],
-        in_specs=[VMEM] * 6,
+        out_shape=[shape((768, NVEC), BF16), shape((1, 3 * FACE, 256), BF16)],
+        in_specs=[VMEM] * 5,
         out_specs=[VMEM] * 2,
         scratch_shapes=[pltpu.VMEM((32, 24, NVEC), F32)],
         compiler_params=params,
-    )(part0, left0, link_wide, *arrived)
+    )(part0, left0, link_wide, arrived[1], early)
     other = lax.ppermute(send, "xyz", [(i, i ^ 1) for i in range(64)])
     keep = pl.pallas_call(
         keep_kernel,
         out_shape=shape((768, NVEC), F32),
-        in_specs=[VMEM] * 3,
+        in_specs=[VMEM] * 4,
         out_specs=VMEM,
         scratch_shapes=[pltpu.VMEM((32, 24, NVEC), F32)],
         compiler_params=params,
-    )(part1, left1, right)
+    )(part1, left1, right, right_y)
     chip = (keep + other.astype(F32)).astype(BF16).reshape(32, 24, NVEC)
     groups = [[2 * c + core for c in range(32)] for core in range(2)]
     got = lax.all_to_all(chip, "xyz", 0, 0, axis_index_groups=groups, tiled=True)

time: 35.7 us -> 35.4 us (level)
  blocking collectives: 16.5 us -> 15.9 us
  waiting for transfers between devices: 0.81 us -> 1.17 us
    all_to_all x1, blocking collectives: 16.5 us -> 15.9 us  [per_device(): lax.all_to_all(chip, 'xyz', 0, 0, axis_index_groups=groups, tiled=True)]
    ppermute x1, starting transfers between devices: 0.6 us -> 0.09 us  [per_device(): other = lax.ppermute(send, 'xyz', [(i, i ^ 1) for i in range(64)])]
    ppermute x1, waiting for transfers between devices: 0.81 us -> 1.16 us  [per_device(): other = lax.ppermute(send, 'xyz', [(i, i ^ 1) for i in range(64)])]
  transfers between devices with their start and end apart: 4 -> 4, of which waited for: 1 -> 1; matrix products, arithmetic and copies ran while one was open for 0% -> 0% of each run, Pallas kernels for 16% -> 17%
where the time goes in v5:
time: 35.4 us; the launch traced here: 35.3 us
  blocking collectives  15.9 us (45%)
  starting transfers between devices  9.85 us (28%)
  Pallas kernels  7.14 us (20%)
  waiting for transfers between devices  1.17 us (3%)
  local copies, waits for them, and re-layouts  1.14 us (3%)
    all_to_all x1, blocking collectives, per_device(): lax.all_to_all(chip, 'xyz', 0, 0, axis_index_groups=groups, tiled=True)  15.9 us
    ppermute x3, starting transfers between devices, per_device(): lax.ppermute(a, 'xyz', s)  9.76 us
    pallas_call x1, Pallas kernels, per_device(): pl.pallas_call(interior_kernel, out_shape=[part, part, shape((54, FACE, N...  2.85 us
    pallas_call x1, Pallas kernels, per_device(): pl.pallas_call(factor_kernel, out_shape=[shape((6, 4, NVEC, 128), F32), s...  2.6 us
    ppermute x1, waiting for transfers between devices, per_device(): other = lax.ppermute(send, 'xyz', [(i, i ^ 1) for i in range(64)])  1.16 us
    unnamed x3, local copies, waits for them, and re-layouts  1.14 us
  transfers between devices with their start and end apart: 4, of which 1 were waited for; matrix products, arithmetic and copies ran while one was open for 0% of the time, Pallas kernels for 17%

profile of v5, /device:TPU:8, one launch (start us, length us, event | category | flops | bytes accessed | tf_op | source)
XLA Modules:
  0.0 35.3 jit_solution(3310150067929697544)
XLA Ops:
  0.0 0.0 copy-start
  0.0 1.1 %copy.8 = bf16[2,3,512,128]{3,2,1,0:T(8,128)(2,1)S(1)} copy(bf16[2,3,512,128]{3,2,1,0:T(8,128)(2,1)} %param.4) | data formatting | bytes 1572864
  1.1 0.2 shard_map.46
  1.3 6.4 %collective-permute-start = (bf16[6,64,128]{2,1,0:T(8,128)(2,1)S(1)}, bf16[6,64,128]{2,1,0:T(8,128)(2,1)S(1)}, u32[]{:S(2)}, u32[]{:S(2)}) collective-permute-start(bf16[6,64,128]{2,1,0:T(8,128)(2,1)S(1)} %get-tuple-element.36), channel_id=1, source_target_pairs={{0,48},{1,49},{2,50},{3,51},{4,52},{5,53},{6,54},{7,55},{8,56},{9,... | collective-permute-start | bytes 294920 | tf_op jit(solution)/shard_map/ppermute | solution.py:301
  7.7 0.7 %collective-permute-start.1 = (bf16[6,64,128]{2,1,0:T(8,128)(2,1)S(1)}, bf16[6,64,128]{2,1,0:T(8,128)(2,1)S(1)}, u32[]{:S(2)}, u32[]{:S(2)}) collective-permute-start(bf16[6,64,128]{2,1,0:T(8,128)(2,1)S(1)} %get-tuple-element.37), channel_id=1, source_target_pairs={{0,3},{1,0},{2,1},{3,2},{4,7},{5,4},{6,5},{7,6},{8,11},{9,8},{10,9... | collective-permute-start | bytes 294920 | tf_op jit(solution)/shard_map/ppermute | solution.py:301
  8.3 2.7 %collective-permute-start.2 = (bf16[6,64,128]{2,1,0:T(8,128)(2,1)S(1)}, bf16[6,64,128]{2,1,0:T(8,128)(2,1)S(1)}, u32[]{:S(2)}, u32[]{:S(2)}) collective-permute-start(bf16[6,64,128]{2,1,0:T(8,128)(2,1)S(1)} %get-tuple-element.39), channel_id=1, source_target_pairs={{0,4},{1,5},{2,6},{3,7},{4,8},{5,9},{6,10},{7,11},{8,12},{9,13},{1... | collective-permute-start | bytes 294920 | tf_op jit(solution)/shard_map/ppermute | solution.py:301
  11.1 0.0 copy-done
  11.1 2.6 %shard_map.47 = (f32[6,4,128,128]{3,2,1,0:T(8,128)S(1)}, bf16[512,1536]{1,0:T(8,128)(2,1)S(1)}, f32[81,8,512]{2,1,0:T(8,128)S(1)}, bf16[3,256,192]{2,1,0:T(8,128...) custom-call(s32[2,3]{1,0:T(2,128)} %mom_hbm.1, s32[3]{0:T(128)} %dir_hbm.1, ...), custom_call_target="tpu_custom_call" | custom-call | tf_op jit(solution)/shard_map/pallas_call | solution.py:304
  13.7 2.9 %shard_map.48 = (f32[6,128,128]{2,1,0:T(8,128)S(1)}, f32[6,128,128]{2,1,0:T(8,128)S(1)}, f32[54,64,128]{2,1,0:T(8,128)S(1)}) custom-call(f32[6,4,128,128]{3,2,1,0:T(8,128)S(1)} %get-tuple-element.27.vt, bf16[512,1536]{1,0:T(8,128)(2,1)S(1)} %get-tuple-element.28.lt, f32[81,8,512]{2,1,0:T(8,128)S(1)} %get-tuple-element.29.ub, ...), custom_call_target="tpu_custom_call" | custom-call | flops 2000000000 | bytes 4000000 | tf_op jit(solution)/shard_map/pallas_call | solution.py:331
  16.5 0.0 collective-permute-done.x_ref
  16.6 0.0 collective-permute-done.1.z_ref
  16.6 0.4 %shard_map.49 = (f32[32,16,128]{2,1,0:T(8,128)S(1)}, bf16[2,192,256]{2,1,0:T(8,128)(2,1)S(1)}) custom-call(f32[6,128,128]{2,1,0:T(8,128)S(1)} %get-tuple-element.33.part_ref, bf16[3,256,192]{2,1,0:T(8,128)(2,1)S(1)} %get-tuple-element.34.lf_ref, f32[54,64,128]{2,1,0:T(8,128)S(1)} %get-tuple-element.35.uf_ref, ...), custom_call_target="tpu_custom_call" | custom-call | tf_op jit(solution)/shard_map/pallas_call | solution.py:342
  16.9 0.0 collective-permute-done.2.y_ref
  17.0 0.3 shard_map.50
  17.2 0.1 collective-permute-start.3
  17.3 0.3 shard_map.51
  17.6 1.2 %collective-permute-done.3 = bf16[768,128]{1,0:T(8,128)(2,1)S(1)} collective-permute-done((bf16[768,128]{1,0:T(8,128)(2,1)S(1)}, bf16[768,128]{1,0:T(8,128)(2,1)S(1)}, u32[]{:S(2)}, u32[]{:S(2)}) %collective-permute-start.3) | collective-permute-done | bytes 196640 | tf_op jit(solution)/shard_map/ppermute | solution.py:357
  18.8 15.9 %all_to_all.5.got_ref = bf16[32,24,128]{2,1,0:T(8,128)(2,1)S(1)} all-to-all(bf16[32,24,128]{2,1,0:T(8,128)(2,1)S(1)} %bitcast.7), channel_id=1, replica_groups={{0,2,4,6,8,10,12,14,16,18,20,22,24,26,28,30,32,34,36,38,40,42,44,46,48,..., dimensions={0} | all-to-all | bytes 393216 | tf_op jit(solution)/shard_map/all_to_all | solution.py:368
  34.6 0.6 %shard_map.52 = f32[2,3,2,2,128]{4,3,2,1,0:T(2,128)} custom-call(s32[3,8,128]{2,1,0:T(8,128)S(1)} %get-tuple-element.26.asked_ref, bf16[32,24,128]{2,1,0:T(8,128)(2,1)S(1)} %all_to_all.5.got_ref), custom_call_target="tpu_custom_call" | custom-call | tf_op jit(solution)/shard_map/pallas_call | solution.py:369
  (1 shorter events, 0.0 us)
Async XLA Ops:
  0.0 11.1 %copy-start = (bf16[3,2,3,3,512]{4,1,3,2,0:T(2,128)(2,1)S(1)}, bf16[3,2,3,3,512]{4,1,3,2,0:T(2,128)(2,1)}, u32[]{:S(2)}) copy-start(bf16[3,2,3,3,512]{4,1,3,2,0:T(2,128)(2,1)} %param.5) | copy-start | bytes 165892
  1.3 15.2 %collective-permute-start = (bf16[6,64,128]{2,1,0:T(8,128)(2,1)S(1)}, bf16[6,64,128]{2,1,0:T(8,128)(2,1)S(1)}, u32[]{:S(2)}, u32[]{:S(2)}) collective-permute-start(bf16[6,64,128]{2,1,0:T(8,128)(2,1)S(1)} %get-tuple-element.36), channel_id=1, source_target_pairs={{0,48},{1,49},{2,50},{3,51},{4,52},{5,53},{6,54},{7,55},{8,56},{9,... | collective-permute-start | bytes 294920 | tf_op jit(solution)/shard_map/ppermute | solution.py:301
  7.7 8.9 %collective-permute-start.1 = (bf16[6,64,128]{2,1,0:T(8,128)(2,1)S(1)}, bf16[6,64,128]{2,1,0:T(8,128)(2,1)S(1)}, u32[]{:S(2)}, u32[]{:S(2)}) collective-permute-start(bf16[6,64,128]{2,1,0:T(8,128)(2,1)S(1)} %get-tuple-element.37), channel_id=1, source_target_pairs={{0,3},{1,0},{2,1},{3,2},{4,7},{5,4},{6,5},{7,6},{8,11},{9,8},{10,9... | collective-permute-start | bytes 294920 | tf_op jit(solution)/shard_map/ppermute | solution.py:301
  8.3 8.6 %collective-permute-start.2 = (bf16[6,64,128]{2,1,0:T(8,128)(2,1)S(1)}, bf16[6,64,128]{2,1,0:T(8,128)(2,1)S(1)}, u32[]{:S(2)}, u32[]{:S(2)}) collective-permute-start(bf16[6,64,128]{2,1,0:T(8,128)(2,1)S(1)} %get-tuple-element.39), channel_id=1, source_target_pairs={{0,4},{1,5},{2,6},{3,7},{4,8},{5,9},{6,10},{7,11},{8,12},{9,13},{1... | collective-permute-start | bytes 294920 | tf_op jit(solution)/shard_map/ppermute | solution.py:301
  17.2 1.5 %collective-permute-start.3 = (bf16[768,128]{1,0:T(8,128)(2,1)S(1)}, bf16[768,128]{1,0:T(8,128)(2,1)S(1)}, u32[]{:S(2)}, u32[]{:S(2)}) collective-permute-start(bf16[768,128]{1,0:T(8,128)(2,1)S(1)} %get-tuple-element.42), channel_id=1, source_target_pairs={{0,1},{1,0},{2,3},{3,2},{4,5},{5,4},{6,7},{7,6},{8,9},{9,8},{10,11... | collective-permute-start | bytes 589832 | tf_op jit(solution)/shard_map/ppermute | solution.py:357

commit v6 on v5

--- a/solution.py
+++ b/solution.py
@@ -253,14 +253,14 @@
         early_ref[:, pl.ds(n * 8, 8), :] = boundary_half(d, part_ref, lf_ref, right_ref[n])
 
 
-def send_kernel(part_ref, lf_ref, uf_ref, y_ref, early_ref, send_ref, right_ref, chunk):
+def send_kernel(x_ref, part_ref, lf_ref, uf_ref, y_ref, early_ref, send_ref, right_ref, chunk):
     face_products(1, uf_ref, y_ref, right_ref, 0)
     chunk[:, pl.ds(0, 16), :] = early_ref[...]
     chunk[:, pl.ds(16, 8), :] = boundary_half(1, part_ref, lf_ref, right_ref[0])
     send_ref[...] = chunk[...].reshape(768, NVEC).astype(BF16)
 
 
-def keep_kernel(part_ref, lf_ref, right_ref, right_y_ref, keep_ref, chunk):
+def keep_kernel(right_y_ref, part_ref, lf_ref, right_ref, keep_ref, chunk):
     for n, d in enumerate((0, 2, 1)):
         right = right_y_ref[0] if d == 1 else right_ref[n]
         chunk[:, pl.ds(n * 8, 8), :] = boundary_half(d, part_ref, lf_ref, right)
@@ -349,11 +349,11 @@
     send, right_y = pl.pallas_call(
         send_kernel,
         out_shape=[shape((768, NVEC), BF16), shape((1, 3 * FACE, 256), BF16)],
-        in_specs=[VMEM] * 5,
+        in_specs=[VMEM] * 6,
         out_specs=[VMEM] * 2,
         scratch_shapes=[pltpu.VMEM((32, 24, NVEC), F32)],
         compiler_params=params,
-    )(part0, left0, link_wide, arrived[1], early)
+    )(arrived[0], part0, left0, link_wide, arrived[1], early)
     other = lax.ppermute(send, "xyz", [(i, i ^ 1) for i in range(64)])
     keep = pl.pallas_call(
         keep_kernel,
@@ -362,7 +362,7 @@
         out_specs=VMEM,
         scratch_shapes=[pltpu.VMEM((32, 24, NVEC), F32)],
         compiler_params=params,
-    )(part1, left1, right, right_y)
+    )(right_y, part1, left1, right)
     chip = (keep + other.astype(F32)).astype(BF16).reshape(32, 24, NVEC)
     groups = [[2 * c + core for c in range(32)] for core in range(2)]
     got = lax.all_to_all(chip, "xyz", 0, 0, axis_index_groups=groups, tiled=True)

time: 35.4 us -> 35.4 us (level)
  waiting for transfers between devices: 1.17 us -> 0.81 us
    ppermute x1, starting transfers between devices: 0.09 us -> 0.6 us  [per_device(): other = lax.ppermute(send, 'xyz', [(i, i ^ 1) for i in range(64)])]
    ppermute x1, waiting for transfers between devices: 1.16 us -> 0.8 us  [per_device(): other = lax.ppermute(send, 'xyz', [(i, i ^ 1) for i in range(64)])]
    ppermute x3, starting transfers between devices: 9.76 us -> 9.4 us  [per_device(): lax.ppermute(a, 'xyz', s)]
where the time goes in v6:
time: 35.4 us; the launch traced here: 35.3 us
  blocking collectives  16.1 us (45%)
  starting transfers between devices  10 us (28%)
  Pallas kernels  7.14 us (20%)
  local copies, waits for them, and re-layouts  1.14 us (3%)
  waiting for transfers between devices  0.81 us (2%)
    all_to_all x1, blocking collectives, per_device(): lax.all_to_all(chip, 'xyz', 0, 0, axis_index_groups=groups, tiled=True)  16.1 us
    ppermute x3, starting transfers between devices, per_device(): lax.ppermute(a, 'xyz', s)  9.4 us
    pallas_call x1, Pallas kernels, per_device(): pl.pallas_call(interior_kernel, out_shape=[part, part, shape((54, FACE, N...  2.85 us
    pallas_call x1, Pallas kernels, per_device(): pl.pallas_call(factor_kernel, out_shape=[shape((6, 4, NVEC, 128), F32), s...  2.6 us
    unnamed x3, local copies, waits for them, and re-layouts  1.14 us
    ppermute x1, waiting for transfers between devices, per_device(): other = lax.ppermute(send, 'xyz', [(i, i ^ 1) for i in range(64)])  0.8 us
  transfers between devices with their start and end apart: 4, of which 1 were waited for; matrix products, arithmetic and copies ran while one was open for 0% of the time, Pallas kernels for 17%

profile of v6, /device:TPU:8, one launch (start us, length us, event | category | flops | bytes accessed | tf_op | source)
XLA Modules:
  0.0 35.3 jit_solution(13744007497007498988)
XLA Ops:
  0.0 0.0 copy-start
  0.0 1.1 %copy.8 = bf16[2,3,512,128]{3,2,1,0:T(8,128)(2,1)S(1)} copy(bf16[2,3,512,128]{3,2,1,0:T(8,128)(2,1)} %param.4) | data formatting | bytes 1572864
  1.1 0.2 shard_map.46
  1.3 6.4 %collective-permute-start = (bf16[6,64,128]{2,1,0:T(8,128)(2,1)S(1)}, bf16[6,64,128]{2,1,0:T(8,128)(2,1)S(1)}, u32[]{:S(2)}, u32[]{:S(2)}) collective-permute-start(bf16[6,64,128]{2,1,0:T(8,128)(2,1)S(1)} %get-tuple-element.27), channel_id=1, source_target_pairs={{0,48},{1,49},{2,50},{3,51},{4,52},{5,53},{6,54},{7,55},{8,56},{9,... | collective-permute-start | bytes 294920 | tf_op jit(solution)/shard_map/ppermute | solution.py:301
  7.7 3.0 %collective-permute-start.1 = (bf16[6,64,128]{2,1,0:T(8,128)(2,1)S(1)}, bf16[6,64,128]{2,1,0:T(8,128)(2,1)S(1)}, u32[]{:S(2)}, u32[]{:S(2)}) collective-permute-start(bf16[6,64,128]{2,1,0:T(8,128)(2,1)S(1)} %get-tuple-element.35), channel_id=1, source_target_pairs={{0,4},{1,5},{2,6},{3,7},{4,8},{5,9},{6,10},{7,11},{8,12},{9,13},{1... | collective-permute-start | bytes 294920 | tf_op jit(solution)/shard_map/ppermute | solution.py:301
  10.7 0.0 collective-permute-start.2
  10.7 0.0 copy-done
  10.7 2.6 %shard_map.47 = (f32[6,4,128,128]{3,2,1,0:T(8,128)S(1)}, bf16[512,1536]{1,0:T(8,128)(2,1)S(1)}, f32[81,8,512]{2,1,0:T(8,128)S(1)}, bf16[3,256,192]{2,1,0:T(8,128...) custom-call(s32[2,3]{1,0:T(2,128)} %mom_hbm.1, s32[3]{0:T(128)} %dir_hbm.1, ...), custom_call_target="tpu_custom_call" | custom-call | tf_op jit(solution)/shard_map/pallas_call | solution.py:304
  13.3 2.9 %shard_map.48 = (f32[6,128,128]{2,1,0:T(8,128)S(1)}, f32[6,128,128]{2,1,0:T(8,128)S(1)}, f32[54,64,128]{2,1,0:T(8,128)S(1)}) custom-call(f32[6,4,128,128]{3,2,1,0:T(8,128)S(1)} %get-tuple-element.28.vt, bf16[512,1536]{1,0:T(8,128)(2,1)S(1)} %get-tuple-element.29.lt, f32[81,8,512]{2,1,0:T(8,128)S(1)} %get-tuple-element.30.ub, ...), custom_call_target="tpu_custom_call" | custom-call | flops 2000000000 | bytes 4000000 | tf_op jit(solution)/shard_map/pallas_call | solution.py:331
  16.2 0.0 collective-permute-done.x_ref
  16.2 0.0 collective-permute-done.2.z_ref
  16.2 0.4 %shard_map.49 = (f32[32,16,128]{2,1,0:T(8,128)S(1)}, bf16[2,192,256]{2,1,0:T(8,128)(2,1)S(1)}) custom-call(f32[6,128,128]{2,1,0:T(8,128)S(1)} %get-tuple-element.32.part_ref, bf16[3,256,192]{2,1,0:T(8,128)(2,1)S(1)} %get-tuple-element.33.lf_ref, f32[54,64,128]{2,1,0:T(8,128)S(1)} %get-tuple-element.34.uf_ref, ...), custom_call_target="tpu_custom_call" | custom-call | tf_op jit(solution)/shard_map/pallas_call | solution.py:342
  16.6 0.0 collective-permute-done.1.y_ref
  16.6 0.3 shard_map.50
  16.9 0.6 %collective-permute-start.3 = (bf16[768,128]{1,0:T(8,128)(2,1)S(1)}, bf16[768,128]{1,0:T(8,128)(2,1)S(1)}, u32[]{:S(2)}, u32[]{:S(2)}) collective-permute-start(bf16[768,128]{1,0:T(8,128)(2,1)S(1)} %get-tuple-element.42), channel_id=1, source_target_pairs={{0,1},{1,0},{2,3},{3,2},{4,5},{5,4},{6,7},{7,6},{8,9},{9,8},{10,11... | collective-permute-start | bytes 589832 | tf_op jit(solution)/shard_map/ppermute | solution.py:357
  17.5 0.3 shard_map.51
  17.7 0.8 %collective-permute-done.3 = bf16[768,128]{1,0:T(8,128)(2,1)S(1)} collective-permute-done((bf16[768,128]{1,0:T(8,128)(2,1)S(1)}, bf16[768,128]{1,0:T(8,128)(2,1)S(1)}, u32[]{:S(2)}, u32[]{:S(2)}) %collective-permute-start.3) | collective-permute-done | bytes 196640 | tf_op jit(solution)/shard_map/ppermute | solution.py:357
  18.6 16.1 %all_to_all.5.got_ref = bf16[32,24,128]{2,1,0:T(8,128)(2,1)S(1)} all-to-all(bf16[32,24,128]{2,1,0:T(8,128)(2,1)S(1)} %bitcast.7), channel_id=1, replica_groups={{0,2,4,6,8,10,12,14,16,18,20,22,24,26,28,30,32,34,36,38,40,42,44,46,48,..., dimensions={0} | all-to-all | bytes 393216 | tf_op jit(solution)/shard_map/all_to_all | solution.py:368
  34.6 0.6 %shard_map.52 = f32[2,3,2,2,128]{4,3,2,1,0:T(2,128)} custom-call(s32[3,8,128]{2,1,0:T(8,128)S(1)} %get-tuple-element.26.asked_ref, bf16[32,24,128]{2,1,0:T(8,128)(2,1)S(1)} %all_to_all.5.got_ref), custom_call_target="tpu_custom_call" | custom-call | tf_op jit(solution)/shard_map/pallas_call | solution.py:369
  (1 shorter events, 0.0 us)
Async XLA Ops:
  0.0 10.7 %copy-start = (bf16[3,2,3,3,512]{4,1,3,2,0:T(2,128)(2,1)S(1)}, bf16[3,2,3,3,512]{4,1,3,2,0:T(2,128)(2,1)}, u32[]{:S(2)}) copy-start(bf16[3,2,3,3,512]{4,1,3,2,0:T(2,128)(2,1)} %param.5) | copy-start | bytes 165892
  1.3 14.9 %collective-permute-start = (bf16[6,64,128]{2,1,0:T(8,128)(2,1)S(1)}, bf16[6,64,128]{2,1,0:T(8,128)(2,1)S(1)}, u32[]{:S(2)}, u32[]{:S(2)}) collective-permute-start(bf16[6,64,128]{2,1,0:T(8,128)(2,1)S(1)} %get-tuple-element.27), channel_id=1, source_target_pairs={{0,48},{1,49},{2,50},{3,51},{4,52},{5,53},{6,54},{7,55},{8,56},{9,... | collective-permute-start | bytes 294920 | tf_op jit(solution)/shard_map/ppermute | solution.py:301
  7.7 8.9 %collective-permute-start.1 = (bf16[6,64,128]{2,1,0:T(8,128)(2,1)S(1)}, bf16[6,64,128]{2,1,0:T(8,128)(2,1)S(1)}, u32[]{:S(2)}, u32[]{:S(2)}) collective-permute-start(bf16[6,64,128]{2,1,0:T(8,128)(2,1)S(1)} %get-tuple-element.35), channel_id=1, source_target_pairs={{0,4},{1,5},{2,6},{3,7},{4,8},{5,9},{6,10},{7,11},{8,12},{9,13},{1... | collective-permute-start | bytes 294920 | tf_op jit(solution)/shard_map/ppermute | solution.py:301
  10.7 5.5 %collective-permute-start.2 = (bf16[6,64,128]{2,1,0:T(8,128)(2,1)S(1)}, bf16[6,64,128]{2,1,0:T(8,128)(2,1)S(1)}, u32[]{:S(2)}, u32[]{:S(2)}) collective-permute-start(bf16[6,64,128]{2,1,0:T(8,128)(2,1)S(1)} %get-tuple-element.36), channel_id=1, source_target_pairs={{0,3},{1,0},{2,1},{3,2},{4,7},{5,4},{6,5},{7,6},{8,11},{9,8},{10,9... | collective-permute-start | bytes 294920 | tf_op jit(solution)/shard_map/ppermute | solution.py:301
  16.9 1.7 %collective-permute-start.3 = (bf16[768,128]{1,0:T(8,128)(2,1)S(1)}, bf16[768,128]{1,0:T(8,128)(2,1)S(1)}, u32[]{:S(2)}, u32[]{:S(2)}) collective-permute-start(bf16[768,128]{1,0:T(8,128)(2,1)S(1)} %get-tuple-element.42), channel_id=1, source_target_pairs={{0,1},{1,0},{2,3},{3,2},{4,5},{5,4},{6,7},{7,6},{8,9},{9,8},{10,11... | collective-permute-start | bytes 589832 | tf_op jit(solution)/shard_map/ppermute | solution.py:357
